TPU v7x, 128 devices: a whole 4x4x4 slice. The times are simulated.
128 devices in a mesh: sec: 8 (over x, z_lo), blk: 16 (over y, z_hi, core).
Axes of the slice: x: 4, y: 4, z: 4 (z_hi: 2, z_lo: 2; z = z_hi * 2 + z_lo), core: 2. Of those that a mesh axis runs over, the one named last changes fastest.
Arguments:
- thermal_kelvin: float32 [2048, 16384], P('sec', 'blk'), may hold values from -6 to 6
- diffusion_factor: float32 [2048, 16384], P('sec', 'blk'), may hold values from 0.15 to 0.6
- speed_lateral: float32 [2048, 16384], P('sec', 'blk'), may hold values from -0.45 to 0.45
- speed_lineward: float32 [2048, 16384], P('sec', 'blk'), may hold values from -0.45 to 0.45
- patch_mesh_slot: int32 [1048576], P(('sec', 'blk')), may hold values from 0 to 262143
- patch_holder_lateral: int32 [1048576, 1], P(('sec', 'blk')), may hold values from 0 to 15; in each aligned block of 8192 rows (0 to 8191, 8192 to 16383, ...) at most 768 rows name the same one
- patch_boundary_dest: int32 [1048576], P(('sec', 'blk')), may hold values from 0 to 262143
- patch_film_factor: float32 [1048576], P(('sec', 'blk')), may hold values from 0.05 to 0.5
- patch_kelvin_prior: float32 [1048576], P(('sec', 'blk')), may hold values from -6 to 6
Outputs:
- new_temperature: float32 [2048, 16384], P('sec', 'blk')
- wall_out: float32 [1048576], P(('sec', 'blk'))
Inputs may be any that keep to these rules, and one draw needn't show every extreme that they name: In every block's 8192 faces at most 768 name one column, and some block has a column named exactly 768 times. On blocks of solid rows patch_holder_lateral and patch_boundary_dest are not read.
All inputs are finite; a program needn't handle non-finite values.
Results may differ from a plain program's by a relative error of at most 0.00002.
Values sent between devices are 32-bit elements; how exact they have to be, the bound alone decides.
A program may use at most 64 MiB of HBM per device.

v0:
```python
import jax
import jax.numpy as jnp
from jax import lax
from jax.sharding import PartitionSpec as P

WROWS = 128
GAS_MINOR_PASSES = 10
SOLID_SUBSTEPS = 4


time_step = 0.2


def extended(block, sides, width):
    for axis, dim in sides:
        count = lax.axis_size(axis)
        forward = [(i, i + 1) for i in range(count - 1)]
        forward.append((count - 1, 0))
        backward = [(target, source) for source, target in forward]
        low = lax.ppermute(
            lax.slice_in_dim(block, block.shape[dim] - width, None, axis=dim), axis, forward
        )
        high = lax.ppermute(lax.slice_in_dim(block, 0, width, axis=dim), axis, backward)
        block = jnp.concatenate([low, block, high], axis=dim)
    return block


def stencil_terms(padded_temp, padded_cond):
    center = padded_temp[1:-1, 1:-1]
    north = padded_temp[2:, 1:-1]
    south = padded_temp[:-2, 1:-1]
    east = padded_temp[1:-1, 2:]
    west = padded_temp[1:-1, :-2]
    kcenter = padded_cond[1:-1, 1:-1]
    spread = 0.5 * (
        (kcenter + padded_cond[2:, 1:-1]) * (north - center)
        + (kcenter + padded_cond[:-2, 1:-1]) * (south - center)
        + (kcenter + padded_cond[1:-1, 2:]) * (east - center)
        + (kcenter + padded_cond[1:-1, :-2]) * (west - center)
    )
    return (center, spread, east - west, north - south)


def fluid_advance(padded_temp, padded_cond, speed_lateral, speed_lineward):
    center, spread, across, upward = stencil_terms(padded_temp, padded_cond)
    return center + time_step * (spread - 0.5 * (speed_lateral * across + speed_lineward * upward))


def solid_advance(padded_temp, padded_cond):
    center, spread, across, upward = stencil_terms(padded_temp, padded_cond)
    return center + time_step * spread


def extend(field_block, low_edge, high_edge):
    padded = extended(field_block, (("sec", 0), ("blk", 1)), 1)
    first_row = jnp.where(low_edge, padded[1:2], padded[0:1])
    last_row = jnp.where(high_edge, padded[-2:-1], padded[-1:])
    return jnp.concatenate([first_row, padded[1:-1], last_row], axis=0)


def body(
    thermal_kelvin,
    diffusion_factor,
    speed_lateral,
    speed_lineward,
    patch_mesh_slot,
    patch_holder_lateral,
    patch_boundary_dest,
    patch_film_factor,
    patch_kelvin_prior,
):
    sections = lax.axis_size("sec")
    columns = lax.axis_size("blk")
    fluid_rows = 3 * sections // 4
    solid_rows = sections - fluid_rows
    section = lax.axis_index("sec")
    is_fluid = section < fluid_rows
    is_solid = jnp.logical_not(is_fluid)
    low_edge = (section == 0) | (section == fluid_rows)
    high_edge = (section == fluid_rows - 1) | (section == sections - 1)
    tile_span = thermal_kelvin.shape
    block_width = tile_span[1]
    cell_count = tile_span[0] * tile_span[1]
    resident_patches = patch_mesh_slot.shape[0]
    capacity = 3 * resident_patches // (2 * columns)
    wall_cells = WROWS * block_width
    padded_cond = extend(diffusion_factor, low_edge, high_edge)
    coef_map = (
        jnp.zeros((cell_count,), jnp.float32)
        .at[patch_mesh_slot]
        .add(patch_film_factor)
        .reshape(tile_span)
    )
    drive_map = (
        jnp.zeros((cell_count,), jnp.float32)
        .at[patch_mesh_slot]
        .add(patch_film_factor * patch_kelvin_prior)
        .reshape(tile_span)
    )

    def gas_pass_number(substep_index, carry):
        combined_state, state_total = carry
        padded_temp = extend(combined_state, low_edge, high_edge)
        advanced = fluid_advance(padded_temp, padded_cond, speed_lateral, speed_lineward)
        stepped = advanced - time_step * (combined_state * coef_map - drive_map)
        return (jnp.where(is_fluid, stepped, combined_state), state_total + combined_state)

    combined_state, state_total = lax.fori_loop(
        0, GAS_MINOR_PASSES, gas_pass_number, (thermal_kelvin, jnp.zeros(tile_span, jnp.float32))
    )
    mean_flux = patch_film_factor * (
        state_total.reshape(-1)[patch_mesh_slot] / GAS_MINOR_PASSES - patch_kelvin_prior
    )
    column_of = patch_holder_lateral[:, 0]
    one_hot = (column_of[:, None] == jnp.arange(columns, dtype=jnp.int32)[None, :]).astype(
        jnp.int32
    )
    slot_index = jnp.sum(jnp.cumsum(one_hot, axis=0) * one_hot, axis=1) - 1
    position = column_of * capacity + slot_index
    sent_flux = jnp.where(is_fluid, mean_flux, 0.0)
    sent_target = jnp.where(is_fluid, patch_boundary_dest.astype(jnp.float32), -1.0)
    outgoing = jnp.stack(
        [
            jnp.zeros((columns * capacity,), jnp.float32).at[position].set(sent_flux),
            jnp.full((columns * capacity,), -1.0, jnp.float32).at[position].set(sent_target),
        ]
    )
    incoming = lax.all_to_all(
        outgoing.reshape(2, columns, capacity), "blk", split_axis=1, concat_axis=1, tiled=True
    ).reshape(2, columns * capacity)
    target_index = incoming[1].astype(jnp.int32)
    is_valid = target_index >= 0
    safe_target = jnp.where(is_valid, target_index, 0)
    solid_index = jnp.clip(section - fluid_rows, 0, solid_rows - 1)
    partial_wall = (
        jnp.zeros((solid_rows * wall_cells,), jnp.float32)
        .at[safe_target]
        .add(jnp.where(is_valid, incoming[0], 0.0))
    )
    all_walls = lax.psum(partial_wall, "sec")
    wall_source = lax.dynamic_slice_in_dim(all_walls, solid_index * wall_cells, wall_cells)
    layer_source = (time_step * wall_source).reshape(WROWS, block_width)
    for substep_index in range(SOLID_SUBSTEPS):
        padded_temp = extend(combined_state, low_edge, high_edge)
        advanced = solid_advance(padded_temp, padded_cond).at[:WROWS].add(layer_source)
        updated = advanced - time_step * (combined_state * coef_map - drive_map)
        combined_state = jnp.where(is_solid, updated, combined_state)
    new_layer = combined_state[:WROWS].reshape(-1)
    placed = lax.dynamic_update_slice_in_dim(
        jnp.zeros((solid_rows * wall_cells,), jnp.float32),
        jnp.where(is_solid, new_layer, 0.0),
        solid_index * wall_cells,
        0,
    )
    wall_table = lax.psum(placed, "sec")
    reply = jnp.where(is_valid, wall_table[safe_target], 0.0).reshape(columns, capacity)
    answer = lax.all_to_all(reply, "blk", split_axis=0, concat_axis=0, tiled=True).reshape(-1)
    wall_out = jnp.where(is_fluid, answer[position], combined_state.reshape(-1)[patch_mesh_slot])
    return (combined_state, wall_out)


def solution(mesh):
    in_specs = (
        P("sec", "blk"),
        P("sec", "blk"),
        P("sec", "blk"),
        P("sec", "blk"),
        P(("sec", "blk")),
        P(("sec", "blk"), None),
        P(("sec", "blk")),
        P(("sec", "blk")),
        P(("sec", "blk")),
    )
    out_specs = (P("sec", "blk"), P(("sec", "blk")))
    return jax.shard_map(body, mesh=mesh, in_specs=in_specs, out_specs=out_specs, check_vma=False)
```

profile of v0, /device:TPU:15, one launch (start us, length us, event | category | flops | bytes accessed | tf_op | source)
XLA Modules:
  0.0 1447.2 jit_solution(10178115685048278853)
XLA Ops:
  24.7 43.6 %scatter_custom_fusion = f32[262144]{0:T(1024)S(1)} fusion(s32[8192]{0:T(1024)} %get-tuple-element.324, f32[8192]{0:T(1024)S(1)} %copy-done.37, f32[]{:T(128)} %constant.147.clone.1), kind=kCustom, calls=%fused_computation.163 | custom fusion | flops 8192 | bytes 1049088 | tf_op jit(solution)/shard_map/scatter-add | solution.py:91
  68.4 44.3 %scatter_custom_fusion.1 = f32[262144]{0:T(1024)} fusion(s32[8192]{0:T(1024)} %get-tuple-element.324, f32[8192]{0:T(1024)} %mul.171, f32[]{:T(128)} %constant.147.clone.1), kind=kCustom, calls=%fused_computation.161 | custom fusion | flops 8192 | bytes 1049088 | tf_op jit(solution)/shard_map/scatter-add | solution.py:97
  123.5 220.7 %while.19 = (s32[]{:T(128)}, f32[256,1024]{1,0:T(8,128)S(1)}, f32[256,1024]{1,0:T(8,128)S(1)}, pred[]{:T(512)}, pred[]{:T(512)}, /*index=5*/f32[256,1024]{1,0:T(...) while((s32[]{:T(128)}, f32[256,1024]{1,0:T(8,128)S(1)}, ...), condition=%wide.region_3.4_spmd.clone, body=%wide.region_2.3_spmd.clone.sunk | while | flops 9967623 | bytes 39993984 | solution.py:108
  128.1 5.3 collective-permute-start.2
  142.5 4.8 fusion.111
  162.8 4.8 fusion.111
  184.6 4.8 fusion.111
  205.4 4.8 fusion.111
  227.6 4.8 fusion.111
  242.3 5.1 collective-permute-done.3
  250.4 4.8 fusion.111
  265.0 5.1 collective-permute-done.3
  273.2 4.8 fusion.111
  287.0 5.1 collective-permute-done.3
  295.2 4.8 fusion.111
  309.0 5.1 collective-permute-done.3
  317.3 4.8 fusion.111
  331.1 5.1 collective-permute-done.3
  346.9 45.5 %gather_fusion = f32[8192]{0:T(1024)S(1)} fusion(f32[262144]{0:T(1024)S(1)} %bitcast.36, s32[8192]{0:T(1024)S(1)} %get-tuple-element.323), kind=kCustom, calls=%fused_computation | custom fusion | bytes 98304 | tf_op jit(solution)/shard_map/gather | solution.py:112
  392.4 30.5 %scatter_custom_fusion.2 = f32[12288]{0:T(1024)S(1)} fusion(s32[8192]{0:T(1024)S(1)} %bitcast.49, f32[8192]{0:T(1024)S(1)} %get-tuple-element.326, f32[]{:T(128)} %constant.147.clone.1), kind=kCustom, calls=%fused_computation.182 | custom fusion | bytes 49156 | tf_op jit(solution)/shard_map/scatter | solution.py:124
  422.9 30.5 %scatter_custom_fusion.3 = f32[12288]{0:T(1024)S(1)} fusion(s32[8192]{0:T(1024)S(1)} %bitcast.50, f32[8192]{0:T(1024)S(1)} %get-tuple-element.325, f32[]{:T(128)} %constant.155.clone.1), kind=kCustom, calls=%fused_computation.180 | custom fusion | bytes 49156 | tf_op jit(solution)/shard_map/scatter | solution.py:125
  454.1 18.8 %all-to-all-start = ((f32[2,16,768]{2,0,1:T(2,128)}), f32[2,16,768]{2,0,1:T(2,128)S(1)}, u32[]{:S(2)}, u32[]{:S(2)}) async-start(f32[2,16,768]{2,0,1:T(2,128)} %pad_maximum_fusion.54), calls=%async_computation | async-start | bytes 196608 | tf_op jit(solution)/shard_map/all_to_all | solution.py:128
  473.6 5.6 all-to-all-done
  479.4 86.3 %scatter_custom_fusion.4 = f32[262144]{0:T(1024)} fusion(s32[12288]{0:T(1024)S(1)} %bitcast.44, f32[12288]{0:T(1024)S(1)} %reshape.288, f32[]{:T(128)} %constant.147.clone.1), kind=kCustom, calls=%fused_computation.159 | custom fusion | flops 12288 | bytes 1048580 | tf_op jit(solution)/shard_map/scatter-add | solution.py:138
  568.8 5.4 collective-permute-done.11
  583.9 52.9 %all-reduce.3.cloned.1.call-done = f32[262144]{0:T(1024)} async-done(((f32[262144]{0:T(1024)}), f32[262144]{0:T(1024)}) %all-reduce.3.cloned.1.call-update) | async-done | bytes 1048592 | tf_op jit(solution)/shard_map/psum | solution.py:140
  650.7 8.4 collective-permute-start.14
  722.7 76.1 %all-reduce.5.cloned.1.call-done = f32[262144]{0:T(1024)} async-done(((f32[262144]{0:T(1024)}), f32[262144]{0:T(1024)}) %all-reduce.5.cloned.1.call-update) | async-done | bytes 1048592 | tf_op jit(solution)/shard_map/psum | solution.py:155
  798.8 536.5 %gather_fusion.1 = f32[12288]{0:T(1024)S(1)} fusion(f32[262144]{0:T(1024)} %all-reduce.5.cloned.1.call-done, s32[12288]{0:T(1024)S(1)} %broadcast_clamp_fusion), kind=kCustom, calls=%fused_computation.1 | custom fusion | bytes 147456 | tf_op jit(solution)/shard_map/gather | solution.py:156
  1336.0 12.3 all-to-all-start.1
  1348.6 45.5 %gather_fusion.3 = f32[8192]{0:T(1024)S(1)} fusion(f32[262144]{0:T(1024)S(1)} %bitcast.37, s32[8192]{0:T(1024)S(1)} %get-tuple-element.323), kind=kCustom, calls=%fused_computation.3 | custom fusion | bytes 98304 | tf_op jit(solution)/shard_map/gather | solution.py:158
  1394.2 45.5 %gather_fusion.2 = f32[8192]{0:T(1024)S(1)} fusion(f32[12288]{0:T(1024)S(1)} %bitcast.35, s32[8192]{0:T(1024)S(1)} %broadcast_clamp_fusion.1), kind=kCustom, calls=%fused_computation.2 | custom fusion | bytes 98304 | tf_op jit(solution)/shard_map/gather | solution.py:158
  (447 shorter events, 269.1 us)
Async XLA Ops:
  8.4 9.3 collective-permute-start.4
  10.1 7.6 collective-permute-start.5
  18.7 97.6 %collective-permute-start.6 = (f32[258,1]{1,0:T(8,128)}, f32[258,1]{1,0:T(8,128)S(1)}, u32[]{:S(2)}, u32[]{:S(2)}) collective-permute-start(f32[258,1]{1,0:T(8,128)} %get-tuple-element.305), channel_id=1, source_target_pairs={{0,1},{1,2},{2,3},{3,4},{4,5},{5,6},{6,7},{7,8},{8,9},{9,10},{10,1... | collective-permute-start | bytes 3104 | tf_op jit(solution)/shard_map/ppermute | solution.py:20
  23.4 92.8 %collective-permute-start.7 = (f32[258,1]{1,0:T(8,128)}, f32[258,1]{1,0:T(8,128)S(1)}, u32[]{:S(2)}, u32[]{:S(2)}) collective-permute-start(f32[258,1]{1,0:T(8,128)} %get-tuple-element.304), channel_id=1, source_target_pairs={{1,0},{2,1},{3,2},{4,3},{5,4},{6,5},{7,6},{8,7},{9,8},{10,9},{11,1... | collective-permute-start | bytes 3104 | tf_op jit(solution)/shard_map/ppermute | solution.py:23
  128.1 7.6 collective-permute-start.2
  133.3 6.0 collective-permute-start.3
  153.5 6.2 collective-permute-start.3
  174.6 6.9 collective-permute-start.3
  195.4 6.9 collective-permute-start.3
  210.4 4.5 collective-permute-start
  217.7 6.9 collective-permute-start.3
  232.6 4.0 collective-permute-start
  233.9 4.2 collective-permute-start.1
  240.0 7.4 collective-permute-start.3
  261.0 4.0 collective-permute-start.2
  262.7 7.4 collective-permute-start.3
  284.7 7.4 collective-permute-start.3
  306.7 7.4 collective-permute-start.3
  327.1 4.0 collective-permute-start.2
  328.8 7.4 collective-permute-start.3
  344.4 128.5 %collective-permute-start.8 = (f32[1,1024]{1,0:T(1,128)S(1)}, f32[1,1024]{1,0:T(1,128)S(1)}, u32[]{:S(2)}, u32[]{:S(2)}) collective-permute-start(f32[1,1024]{1,0:T(1,128)S(1)} %get-tuple-element.314), channel_id=1, source_target_pairs={{0,16},{16,32},{32,48},{48,64},{64,80},{80,96},{96,112},{112,0},{1... | collective-permute-start | bytes 12296 | tf_op jit(solution)/shard_map/ppermute | solution.py:20
  345.8 127.2 %collective-permute-start.9 = (f32[1,1024]{1,0:T(1,128)S(1)}, f32[1,1024]{1,0:T(1,128)S(1)}, u32[]{:S(2)}, u32[]{:S(2)}) collective-permute-start(f32[1,1024]{1,0:T(1,128)S(1)} %get-tuple-element.315), channel_id=1, source_target_pairs={{16,0},{32,16},{48,32},{64,48},{80,64},{96,80},{112,96},{0,112},{1... | collective-permute-start | bytes 12296 | tf_op jit(solution)/shard_map/ppermute | solution.py:23
  454.1 25.0 %all-to-all-start = ((f32[2,16,768]{2,0,1:T(2,128)}), f32[2,16,768]{2,0,1:T(2,128)S(1)}, u32[]{:S(2)}, u32[]{:S(2)}) async-start(f32[2,16,768]{2,0,1:T(2,128)} %pad_maximum_fusion.54), calls=%async_computation | async-start | bytes 196608 | tf_op jit(solution)/shard_map/all_to_all | solution.py:128
  472.9 163.9 %all-reduce.3.cloned.1.call-start = ((), (), s32[]{:S(2)}) async-start(), calls=%async_computation.2 | async-start | bytes 2097152 | tf_op jit(solution)/shard_map/psum | solution.py:140
  565.7 233.1 %all-reduce.5.cloned.1.call-start = ((), (), s32[]{:S(2)}) async-start(), calls=%async_computation.3 | async-start | bytes 2097152 | tf_op jit(solution)/shard_map/psum | solution.py:155
  566.8 7.4 collective-permute-start.11
  650.7 10.4 collective-permute-start.14
  659.1 5.9 collective-permute-start.15
  672.9 4.1 collective-permute-start.16
  681.9 6.2 collective-permute-start.19
  703.3 6.5 collective-permute-start.23
  1336.0 58.1 %all-to-all-start.1 = ((f32[16,1,768]{2,1,0:T(1,128)}), f32[16,1,768]{2,1,0:T(1,128)S(1)}, u32[]{:S(2)}, u32[]{:S(2)}) async-start(f32[16,1,768]{2,1,0:T(1,128)} %copy.14), calls=%async_computation.1 | async-start | bytes 98304 | tf_op jit(solution)/shard_map/all_to_all | solution.py:157
  (118 other events, 1276.5 us)
Sparse Core Ops, SparseCore 0:
  565.8 70.9 all-reduce.2
  722.8 75.9 all-reduce.4
where the time goes:
time: 1460 us; the launch traced here: 1450 us
  local copies, waits for them, and re-layouts  813 us (56%)
  other arithmetic  262 us (18%)
  waiting for transfers between devices  255 us (17%)
  starting transfers between devices  101 us (7%)
  between operations  14.9 us (1%)
    gather x2, local copies, waits for them, and re-layouts, body(): wall_table[safe_target]  537 us
    scatter-add x1, other arithmetic, body(): partial_wall = jnp.zeros((solid_rows * wall_cells,), jnp.float32).at[safe...  86.3 us
    ppermute x30, waiting for transfers between devices, extended(): lax.ppermute(lax.slice_in_dim(block, 0, width, axis=dim), axis, backward)  79.5 us
    psum x1, waiting for transfers between devices, body(): wall_table = lax.psum(placed, 'sec')  76.1 us
    ppermute x30, starting transfers between devices, extended(): lax.ppermute(lax.slice_in_dim(block, block.shape[dim] - width, None, axis...  61 us
    psum x1, waiting for transfers between devices, body(): all_walls = lax.psum(partial_wall, 'sec')  52.9 us
    select_n x10, other arithmetic, gas_pass_number(): jnp.where(is_fluid, stepped, combined_state)  48.2 us
    gather x1, local copies, waits for them, and re-layouts, body(): answer[position]  45.5 us
  transfers between devices with their start and end apart: 64, of which 57 were waited for; matrix products, arithmetic and copies ran while one was open for 18% of the time, Pallas kernels for 0%

commit v1 on v0

v1 whole, which is shorter than its diff:
```python
import functools

import jax
import jax.numpy as jnp
from jax import lax
from jax.experimental import pallas as pl
from jax.experimental.pallas import tpu as pltpu
from jax.sharding import PartitionSpec as P

F32, BF16, I32 = jnp.float32, jnp.bfloat16, jnp.int32
MESH = pl.DeviceIdType.MESH
NT = (((1,), (1,)), ((), ()))

CY, CX = 256, 1024
FACES = 8192
FLUID_ROWS, SECS, COLS = 6, 8, 16
FLUID_STEPS, SOLID_STEPS = 10, 4
DT = 0.2
KB = 512
NB = FACES // KB
BROWS = 8
SLOTS = COLS * BROWS
PAIRS = 56
CROWS = 2 * PAIRS
ALLP = FLUID_ROWS * PAIRS
QUAD = 4
LIST = ALLP + QUAD
HY, HX = 304, 1280
OY, OX = 24, 128
VLIM = 60 << 20


def params(**kw):
    return pltpu.CompilerParams(vmem_limit_bytes=VLIM, **kw)


def iota(shape, dim):
    return lax.broadcasted_iota(I32, shape, dim)


def split2(x):
    hi = x.astype(BF16).astype(F32)
    return hi, (x - hi).astype(BF16).astype(F32)


def onehot(mask):
    return jnp.where(mask, 1.0, 0.0).astype(BF16)


def dot(a, b):
    return jnp.dot(a, b, preferred_element_type=F32)


def dot_nt(a, b):
    return lax.dot_general(a, b, NT, preferred_element_type=F32)


def lane_row(ref, b, n):
    return jnp.concatenate([ref[pl.ds(n * b + i, 1), :] for i in range(n)], axis=1)


def put_lane_row(ref, b, n, v):
    for i in range(n):
        ref[pl.ds(n * b + i, 1), :] = v[:, i * 128:(i + 1) * 128]


def ranks(groups_of, nb, ng, o_ref, p_ref):
    def build(b, _):
        o_ref[pl.ds(pl.multiple_of(b * ng, 8), ng), :] = jnp.where(iota((ng, KB), 0) == groups_of(b), 1.0, 0.0)
        return 0
    lax.fori_loop(0, nb, build, 0)
    before = onehot(iota((KB, KB), 0) < iota((KB, KB), 1))
    o = o_ref[...].astype(BF16)
    p_ref[...] = dot(o, before)
    return dot(o, onehot(iota((KB, 128), 0) >= 0))


def spread_rows(pos, pieces, rows):
    hit = iota((rows, KB), 0) == (pos >> 7)
    a = jnp.concatenate([jnp.where(hit, v, 0.0).astype(BF16) for v in pieces], axis=0)
    c = onehot(iota((128, KB), 0) == (pos & 127))
    return dot_nt(a, c)


def pick(vt, pos, rows):
    r = onehot(iota((rows, KB), 0) == (pos >> 7))
    g = dot(vt, jnp.concatenate([r, r], axis=0))
    return jnp.sum(jnp.where(iota((128, KB), 0) == (pos & 127), g, 0.0), axis=0, keepdims=True)


def transposed_parts(v):
    hi, lo = split2(v.T)
    return jnp.concatenate([hi, lo], axis=1).astype(BF16)


def target_parts(t):
    return (t >> 10).astype(F32), ((t >> 5) & 31).astype(F32), (t & 31).astype(F32)


def target_join(x, rows):
    return (x[0:rows] * 1024.0 + x[rows:2 * rows] * 32.0 + x[2 * rows:3 * rows]).astype(I32)


def prep_kernel(slot, coef, prior, lateral, dest, cm, dm, pos1, tb, acc, o_ref, p_ref):
    acc[...] = jnp.zeros_like(acc)

    def maps(b, _):
        s, c = slot[b], coef[b]
        parts = split2(c) + split2(c * prior[b])
        hit = iota((CY, KB), 0) == (s >> 10)
        a = jnp.concatenate([jnp.where(hit, v, 0.0).astype(BF16) for v in parts], axis=0)
        acc[...] += dot_nt(a, onehot(iota((CX, KB), 0) == (s & 1023)))
        return 0

    lax.fori_loop(0, NB, maps, 0)
    cm[...] = acc[0:CY] + acc[CY:2 * CY]
    dm[...] = acc[2 * CY:3 * CY] + acc[3 * CY:4 * CY]

    @pl.when(lax.axis_index("sec") < FLUID_ROWS)
    def _():
        totals = ranks(lambda b: lateral[b], NB, COLS, o_ref, p_ref)
        carry = jnp.zeros((COLS, 128), F32)
        out = jnp.zeros((3 * SLOTS, 128), F32)
        for b in range(NB):
            rows = slice(b * COLS, (b + 1) * COLS)
            place = p_ref[rows] + jnp.concatenate([carry] * (KB // 128), axis=1)
            rank = jnp.sum(o_ref[rows] * place, axis=0, keepdims=True)
            pos = lateral[b] * (BROWS * 128) + rank.astype(I32)
            pos1[b] = pos
            carry = carry + totals[rows]
            out = out + spread_rows(pos, target_parts(dest[b] + 1024), SLOTS)
        tb[...] = target_join(out, SLOTS)

    @pl.when(lax.axis_index("sec") >= FLUID_ROWS)
    def _():
        pos1[...] = jnp.zeros_like(pos1)
        tb[...] = jnp.zeros_like(tb)


def prep(slot, coef, prior, lateral, dest):
    return pl.pallas_call(
        prep_kernel,
        out_shape=[jax.ShapeDtypeStruct((CY, CX), F32)] * 2
        + [jax.ShapeDtypeStruct((NB, 1, KB), I32), jax.ShapeDtypeStruct((SLOTS, 128), I32)],
        scratch_shapes=[pltpu.VMEM((4 * CY, CX), F32), pltpu.VMEM((NB * COLS, KB), F32), pltpu.VMEM((NB * COLS, KB), F32)],
        compiler_params=params(),
    )(slot, coef, prior, lateral, dest)


def compact_kernel(t, pos2, t2, o_ref, p_ref):
    nb, ng = SLOTS // 4, 8

    @pl.when(lax.axis_index("sec") < FLUID_ROWS)
    def _():
        def group(b):
            v = lane_row(t, b, 4)
            return jnp.where(v >= 1024, ((v - 1024) >> 17) * 4 + ((v >> 8) & 3), -1)

        totals = ranks(group, nb, ng, o_ref, p_ref)
        count = jnp.zeros((ng, 128), F32)
        for b in range(nb):
            count = count + totals[b * ng:(b + 1) * ng]
        units = ((count.astype(I32) + 255) >> 8).astype(F32).astype(BF16)
        lower = onehot(iota((ng, ng), 1) < iota((ng, ng), 0))
        carry = dot(lower, units) * 256.0
        out = jnp.zeros((3 * CROWS, 128), F32)
        for b in range(nb):
            rows = slice(b * ng, (b + 1) * ng)
            place = p_ref[rows] + jnp.concatenate([carry] * (KB // 128), axis=1)
            rank = jnp.sum(o_ref[rows] * place, axis=0, keepdims=True)
            v = lane_row(t, b, 4)
            pos = jnp.where(v >= 1024, rank.astype(I32), -1)
            pos2[b] = pos
            carry = carry + totals[rows]
            out = out + spread_rows(pos, target_parts(v), CROWS)
        t2[...] = target_join(out, CROWS)

    @pl.when(lax.axis_index("sec") >= FLUID_ROWS)
    def _():
        pos2[...] = jnp.zeros_like(pos2)
        t2[...] = jnp.zeros_like(t2)


def compact(t):
    nb = SLOTS // 4
    return pl.pallas_call(
        compact_kernel,
        out_shape=[jax.ShapeDtypeStruct((nb, 1, KB), I32), jax.ShapeDtypeStruct((CROWS, 128), I32)],
        scratch_shapes=[pltpu.VMEM((nb * 8, KB), F32), pltpu.VMEM((nb * 8, KB), F32)],
        compiler_params=params(),
    )(t)


def list_kernel(first, counts, lists):
    sec = lax.axis_index("sec")
    for g in range(4):
        counts[g] = 0

    @pl.when(sec >= FLUID_ROWS)
    def _():
        mine = sec - FLUID_ROWS

        def one(p, _):
            v = first[p]

            @pl.when((v >= 1024) & (((v - 1024) >> 17) == mine))
            def _():
                g = (v >> 8) & 3
                n = counts[g]
                lists[g, n] = p
                counts[g] = n + 1
            return 0

        lax.fori_loop(0, ALLP, one, 0)
        for g in range(4):
            n = counts[g]
            for i in range(QUAD):
                lists[g, n + i] = ALLP


def make_lists(first):
    return pl.pallas_call(
        list_kernel,
        in_specs=[pl.BlockSpec(memory_space=pltpu.SMEM)],
        out_specs=[pl.BlockSpec(memory_space=pltpu.SMEM)] * 2,
        out_shape=[jax.ShapeDtypeStruct((4,), I32), jax.ShapeDtypeStruct((4, LIST), I32)],
        compiler_params=params(),
    )(first)


def pair_row(ref, lists, g, i):
    rows = []
    for j in range(QUAD):
        p = lists[g, QUAD * i + j]
        rows += [ref[pl.ds(2 * p, 1), :], ref[pl.ds(2 * p + 1, 1), :]]
    return jnp.concatenate(rows, axis=1)


def advance(e, c, add, src, dst, k, total):
    r = pl.multiple_of(8 * k, 8)
    x = e[src, pl.ds(r - 8, 24), :]
    mid = x[8:16]
    rows = pl.ds(r, 8)
    if total is not None:
        total[rows, :] += mid[:, OX:OX + CX]
    e[dst, rows, :] = (
        c[4, rows, :] * mid
        + c[0, rows, :] * x[9:17]
        + c[1, rows, :] * x[7:15]
        + c[2, rows, :] * pltpu.roll(mid, HX - 1, 1)
        + c[3, rows, :] * pltpu.roll(mid, 1, 1)
        + c[5, rows, :]
    )


def coefficients(e, c, low, high, k):
    r = pl.multiple_of(8 * k, 8)
    rows = pl.ds(r, 8)
    x = e[1, pl.ds(r - 8, 24), :]
    kc, kn, ks = x[8:16], x[9:17], x[7:15]
    ke, kw = pltpu.roll(kc, HX - 1, 1), pltpu.roll(kc, 1, 1)
    vx, vy = (0.5 * DT) * e[2, rows, :], (0.5 * DT) * e[3, rows, :]
    hn, hs, he, hw = ((0.5 * DT) * (kc + v) for v in (kn, ks, ke, kw))
    an, as_ = hn - vy, hs + vy
    c0 = 1.0 - (hn + hs + he + hw) - DT * e[4, rows, :]
    at = r + iota((8, HX), 0)
    first, last = low & (at == OY), high & (at == OY + CY - 1)
    c0 = c0 + jnp.where(first, as_, 0.0) + jnp.where(last, an, 0.0)
    c[0, rows, :] = jnp.where(last, 0.0, an)
    c[1, rows, :] = jnp.where(first, 0.0, as_)
    c[2, rows, :] = he - vx
    c[3, rows, :] = hw + vx
    c[4, rows, :] = c0
    c[5, rows, :] = DT * e[5, rows, :]


def fluid_kernel(temp, cond, vx, vy, cm, dm, t_out, s_out, ext, e, c, total, pack, land, send, recv, local):
    sec, blk = lax.axis_index("sec"), lax.axis_index("blk")
    fluid = sec < FLUID_ROWS
    low = (sec == 0) | (sec == FLUID_ROWS)
    high = (sec == FLUID_ROWS - 1) | (sec == SECS - 1)
    left, right = lax.rem(blk + COLS - 1, COLS), lax.rem(blk + 1, COLS)
    bar = pltpu.get_barrier_semaphore()

    def signal(to):
        pl.semaphore_signal(bar, inc=1, device_id=to, device_id_type=MESH)

    signal((sec, left))
    signal((sec, right))

    @pl.when(jnp.logical_not(low))
    def _():
        signal((sec - 1, blk))

    @pl.when(jnp.logical_not(high))
    def _():
        signal((sec + 1, blk))

    mid_y, mid_x = slice(OY, OY + CY), slice(OX, OX + CX)
    e[0, mid_y, mid_x] = temp[...]
    e[1, mid_y, mid_x] = cond[...]
    keep = jnp.where(fluid, 1.0, 0.0)
    e[2, mid_y, mid_x] = vx[...] * keep
    e[3, mid_y, mid_x] = vy[...] * keep
    e[4, mid_y, mid_x] = cm[...]
    e[5, mid_y, mid_x] = dm[...]
    total[...] = jnp.zeros_like(total)

    pl.semaphore_wait(bar, 4 - low.astype(I32) - high.astype(I32))

    def rows_copy(src, dst, i, to):
        return pltpu.make_async_remote_copy(
            e.at[pl.ds(0, 6), pl.ds(src, 16), pl.ds(OX, CX)], e.at[pl.ds(0, 6), pl.ds(dst, 16), pl.ds(OX, CX)],
            send.at[i], recv.at[i], device_id=to, device_id_type=MESH)

    to_low = rows_copy(OY, OY + CY, 0, (sec - 1, blk))
    to_high = rows_copy(OY + CY - 16, OY - 16, 1, (sec + 1, blk))

    @pl.when(jnp.logical_not(low))
    def _():
        to_low.start()

    @pl.when(jnp.logical_not(high))
    def _():
        to_high.start()

    @pl.when(low)
    def _():
        for a in range(6):
            e[a, OY - 16:OY, mid_x] = jnp.zeros((16, CX), F32)

    @pl.when(high)
    def _():
        for a in range(6):
            e[a, OY + CY:OY + CY + 16, mid_x] = jnp.zeros((16, CX), F32)

    @pl.when(jnp.logical_not(low))
    def _():
        to_low.wait_send()
        to_high.wait_recv()

    @pl.when(jnp.logical_not(high))
    def _():
        to_high.wait_send()
        to_low.wait_recv()

    lane = iota((8, 128), 1)

    def pack_strip(k, _):
        rows = pl.ds(pl.multiple_of(8 * k, 8), 8)
        lo = jnp.zeros((8, 128), F32)
        hi = jnp.zeros((8, 128), F32)
        for a in range(6):
            here = (lane >> 4) == a
            lo = jnp.where(here, pltpu.roll(e[a, rows, OX:OX + 128], 16 * a, 1), lo)
            hi = jnp.where(here, pltpu.roll(e[a, rows, OX + CX - 128:OX + CX], 16 * a + 16, 1), hi)
        pack[0, rows, :] = lo
        pack[1, rows, :] = hi
        return 0

    lax.fori_loop(1, 37, pack_strip, 0)

    def cols_copy(i, to):
        return pltpu.make_async_remote_copy(
            pack.at[i], land.at[i], send.at[2 + i], recv.at[2 + i], device_id=to, device_id_type=MESH)

    to_left, to_right = cols_copy(0, (sec, left)), cols_copy(1, (sec, right))
    to_left.start()
    to_right.start()
    to_left.wait()
    to_right.wait()

    def unpack_strip(k, _):
        rows = pl.ds(pl.multiple_of(8 * k, 8), 8)
        lo, hi = land[0, rows, :], land[1, rows, :]
        for a in range(6):
            e[a, rows, OX + CX:] = pltpu.roll(lo, (128 - 16 * a) % 128, 1)
            e[a, rows, 0:OX] = pltpu.roll(hi, 112 - 16 * a, 1)
        return 0

    lax.fori_loop(1, 37, unpack_strip, 0)

    def coef_strip(k, _):
        coefficients(e, c, low, high, k)
        return 0

    lax.fori_loop(1, 37, coef_strip, 0)

    @pl.when(fluid)
    def _():
        def step(n, _):
            src = lax.rem(n, 2) * 6

            def strip(k, _):
                advance(e, c, None, src, 6 - src, k, total)
                return 0

            lax.fori_loop(jnp.where(n == 0, 1, 2), jnp.where(n == 0, 37, 36), strip, 0)
            return 0

        lax.fori_loop(0, FLUID_STEPS, step, 0)
        t_out[...] = e[0, mid_y, mid_x]
        s_out[...] = total[mid_y, :]

    @pl.when(jnp.logical_not(fluid))
    def _():
        first = pltpu.make_async_copy(e.at[0], ext.at[0], local.at[0])
        rest = pltpu.make_async_copy(c, ext.at[pl.ds(1, 6)], local.at[1])
        first.start()
        rest.start()
        t_out[...] = jnp.zeros_like(t_out)
        s_out[...] = jnp.zeros_like(s_out)
        first.wait()
        rest.wait()


def fluid(temp, cond, vx, vy, cm, dm):
    return pl.pallas_call(
        fluid_kernel,
        out_shape=[jax.ShapeDtypeStruct((CY, CX), F32)] * 2 + [jax.ShapeDtypeStruct((7, HY, HX), F32)],
        in_specs=[pl.BlockSpec(memory_space=pltpu.VMEM)] * 6,
        out_specs=[pl.BlockSpec(memory_space=pltpu.VMEM)] * 2 + [pl.BlockSpec(memory_space=pl.ANY)],
        scratch_shapes=[
            pltpu.VMEM((7, HY, HX), F32), pltpu.VMEM((6, HY, HX), F32), pltpu.VMEM((HY, CX), F32),
            pltpu.VMEM((2, HY, 128), F32), pltpu.VMEM((2, HY, 128), F32),
            pltpu.SemaphoreType.DMA((4,)), pltpu.SemaphoreType.DMA((4,)), pltpu.SemaphoreType.DMA((2,)),
        ],
        compiler_params=params(collective_id=0, has_side_effects=True),
    )(temp, cond, vx, vy, cm, dm)


def gather_cells(state, st):
    hi, lo = split2(state.T)
    st[:, 0:CY] = hi.astype(BF16)
    st[:, CY:2 * CY] = lo.astype(BF16)


def cell_values(st, s):
    r = onehot(iota((CY, KB), 0) == (s >> 10))
    g = dot(st[...], jnp.concatenate([r, r], axis=0))
    tile = (s & 1023) >> 7
    a = g[0:128]
    for i in range(1, CX // 128):
        a = jnp.where(tile == i, g[128 * i:128 * i + 128], a)
    return jnp.sum(jnp.where(iota((128, KB), 0) == (s & 127), a, 0.0), axis=0, keepdims=True)


def flux_kernel(total, slot, coef, prior, pos1, out, st):
    @pl.when(lax.axis_index("sec") < FLUID_ROWS)
    def _():
        gather_cells(total[...], st)
        out[...] = jnp.zeros_like(out)

        def one(b, _):
            flux = coef[b] * (cell_values(st, slot[b]) * (1.0 / FLUID_STEPS) - prior[b])
            x = spread_rows(pos1[b], split2(flux), SLOTS)
            out[...] += x[0:SLOTS] + x[SLOTS:2 * SLOTS]
            return 0

        lax.fori_loop(0, NB, one, 0)

    @pl.when(lax.axis_index("sec") >= FLUID_ROWS)
    def _():
        out[...] = jnp.zeros_like(out)


def face_flux(total, slot, coef, prior, pos1):
    return pl.pallas_call(
        flux_kernel,
        out_shape=jax.ShapeDtypeStruct((SLOTS, 128), F32),
        scratch_shapes=[pltpu.VMEM((CX, 2 * CY), BF16)],
        compiler_params=params(),
    )(total, slot, coef, prior, pos1)


def second_kernel(flux, pos2, out):
    out[...] = jnp.zeros_like(out)

    @pl.when(lax.axis_index("sec") < FLUID_ROWS)
    def _():
        def one(b, _):
            x = spread_rows(pos2[b], split2(lane_row(flux, b, 4)), CROWS)
            out[...] += x[0:CROWS] + x[CROWS:2 * CROWS]
            return 0

        lax.fori_loop(0, SLOTS // 4, one, 0)


def second(flux, pos2):
    return pl.pallas_call(
        second_kernel,
        out_shape=jax.ShapeDtypeStruct((CROWS, 128), F32),
        compiler_params=params(),
    )(flux, pos2)


def source_kernel(counts, lists, t, f, out, acc):
    sec = lax.axis_index("sec")

    @pl.when(sec >= FLUID_ROWS)
    def _():
        base = 128 * (sec - FLUID_ROWS) + 1
        n = QUAD * 256
        for g in range(4):
            acc[...] = jnp.zeros_like(acc)

            def one(i, _):
                v = pair_row(t, lists, g, i)
                hi, lo = split2(pair_row(f, lists, g, i))
                hit = iota((128, n), 0) == (v >> 10) - base
                a = jnp.concatenate([jnp.where(hit, p, 0.0).astype(BF16) for p in (hi, lo)], axis=0)
                acc[...] += dot_nt(a, onehot(iota((256, n), 0) == (v & 255)))
                return 0

            lax.fori_loop(0, (counts[g] + QUAD - 1) // QUAD, one, 0)
            out[:, 256 * g:256 * (g + 1)] = acc[0:128] + acc[128:256]

    @pl.when(sec < FLUID_ROWS)
    def _():
        out[...] = jnp.zeros_like(out)


def wall_source(counts, lists, t, f):
    return pl.pallas_call(
        source_kernel,
        in_specs=[pl.BlockSpec(memory_space=pltpu.SMEM)] * 2 + [pl.BlockSpec(memory_space=pltpu.VMEM)] * 2,
        out_shape=jax.ShapeDtypeStruct((128, CX), F32),
        scratch_shapes=[pltpu.VMEM((256, 256), F32)],
        compiler_params=params(),
    )(counts, lists, t, f)


def wall_kernel(counts, lists, t, state, out):
    sec = lax.axis_index("sec")
    out[...] = jnp.zeros_like(out)

    @pl.when(sec >= FLUID_ROWS)
    def _():
        base = 128 * (sec - FLUID_ROWS) + 1
        n = QUAD * 256
        for g in range(4):
            table = transposed_parts(state[:, 256 * g:256 * (g + 1)])

            def one(i, _):
                v = pair_row(t, lists, g, i)
                r = onehot(iota((128, n), 0) == (v >> 10) - base)
                x = dot(table, jnp.concatenate([r, r], axis=0))
                x = jnp.where(((v >> 7) & 1) == 1, x[128:256], x[0:128])
                x = jnp.sum(jnp.where(iota((128, n), 0) == (v & 127), x, 0.0), axis=0, keepdims=True)
                for j in range(QUAD):
                    p = lists[g, QUAD * i + j]
                    out[pl.ds(2 * p, 1), :] = x[:, 256 * j:256 * j + 128]
                    out[pl.ds(2 * p + 1, 1), :] = x[:, 256 * j + 128:256 * j + 256]
                return 0

            lax.fori_loop(0, (counts[g] + QUAD - 1) // QUAD, one, 0)


def wall_values(counts, lists, t, state):
    return pl.pallas_call(
        wall_kernel,
        in_specs=[pl.BlockSpec(memory_space=pltpu.SMEM)] * 2 + [pl.BlockSpec(memory_space=pltpu.VMEM)] * 2,
        out_shape=jax.ShapeDtypeStruct((2 * ALLP + 8, 128), F32),
        compiler_params=params(),
    )(counts, lists, t, state)


def solid_kernel(source, t_fluid, ext, t_out, e, c, x, pack, land, send, recv, local):
    sec, blk = lax.axis_index("sec"), lax.axis_index("blk")
    solid = sec >= FLUID_ROWS
    mid_y, mid_x = slice(OY, OY + CY), slice(OX, OX + CX)

    @pl.when(jnp.logical_not(solid))
    def _():
        t_out[...] = t_fluid[...]

    @pl.when(solid)
    def _():
        left, right = lax.rem(blk + COLS - 1, COLS), lax.rem(blk + 1, COLS)
        other = 2 * FLUID_ROWS + 1 - sec
        bar = pltpu.get_barrier_semaphore()
        for to in ((sec, left), (sec, right), (other, blk)):
            pl.semaphore_signal(bar, inc=1, device_id=to, device_id_type=MESH)
        first = pltpu.make_async_copy(ext.at[0], e.at[0], local.at[0])
        rest = pltpu.make_async_copy(ext.at[pl.ds(1, 6)], c, local.at[1])
        first.start()
        rest.start()
        x[0:OY] = jnp.zeros((OY, HX), F32)
        x[OY + 128:OY + CY] = jnp.zeros((CY - 128, HX), F32)
        x[OY:OY + 128, mid_x] = DT * source[...]

        @pl.when(sec == SECS - 1)
        def _():
            x[OY + CY:] = jnp.zeros((HY - OY - CY, HX), F32)

        pl.semaphore_wait(bar, 3)
        up = pltpu.make_async_remote_copy(
            x.at[pl.ds(OY, 16), pl.ds(OX, CX)], x.at[pl.ds(OY + CY, 16), pl.ds(OX, CX)],
            send.at[2], recv.at[2], device_id=(other, blk), device_id_type=MESH)

        @pl.when(sec == SECS - 1)
        def _():
            up.start()
            up.wait_send()

        @pl.when(sec == FLUID_ROWS)
        def _():
            up.wait_recv()

        for at, fro, size in ((0, OY, 128), (128, OY + CY, 16)):
            pack[0, at:at + size] = x[fro:fro + size, OX:OX + 128]
            pack[1, at:at + size] = x[fro:fro + size, OX + CX - 128:OX + CX]

        def cols_copy(i, to):
            return pltpu.make_async_remote_copy(
                pack.at[i], land.at[i], send.at[i], recv.at[i], device_id=to, device_id_type=MESH)

        to_left, to_right = cols_copy(0, (sec, left)), cols_copy(1, (sec, right))
        to_left.start()
        to_right.start()
        to_left.wait()
        to_right.wait()
        for at, fro, size in ((0, OY, 128), (128, OY + CY, 16)):
            x[fro:fro + size, OX + CX:] = land[0, at:at + size]
            x[fro:fro + size, 0:OX] = land[1, at:at + size]
        first.wait()
        rest.wait()

        def drive(k, _):
            rows = pl.ds(pl.multiple_of(8 * k, 8), 8)
            c[5, rows, :] += x[rows, :]
            return 0

        lax.fori_loop(2, 36, drive, 0)

        def step(n, _):
            src = lax.rem(n, 2)

            def strip(k, _):
                advance(e, c, None, src, 1 - src, k, None)
                return 0

            lax.fori_loop(2, 36, strip, 0)
            return 0

        lax.fori_loop(0, SOLID_STEPS, step, 0)
        t_out[...] = e[0, mid_y, mid_x]


def solid_steps(source, t_fluid, ext):
    return pl.pallas_call(
        solid_kernel,
        out_shape=jax.ShapeDtypeStruct((CY, CX), F32),
        in_specs=[pl.BlockSpec(memory_space=pltpu.VMEM)] * 2 + [pl.BlockSpec(memory_space=pl.ANY)],
        out_specs=pl.BlockSpec(memory_space=pltpu.VMEM),
        scratch_shapes=[
            pltpu.VMEM((2, HY, HX), F32), pltpu.VMEM((6, HY, HX), F32), pltpu.VMEM((HY, HX), F32),
            pltpu.VMEM((2, 144, 128), F32), pltpu.VMEM((2, 144, 128), F32),
            pltpu.SemaphoreType.DMA((3,)), pltpu.SemaphoreType.DMA((3,)), pltpu.SemaphoreType.DMA((2,)),
        ],
        compiler_params=params(collective_id=1, has_side_effects=True),
    )(source, t_fluid, ext)


def back_kernel(v, pos2, out):
    out[...] = jnp.zeros_like(out)

    @pl.when(lax.axis_index("sec") < FLUID_ROWS)
    def _():
        vt = transposed_parts(v[0] + v[1])

        def one(b, _):
            put_lane_row(out, b, 4, pick(vt, pos2[b], CROWS))
            return 0

        lax.fori_loop(0, SLOTS // 4, one, 0)


def back(v, pos2):
    return pl.pallas_call(
        back_kernel,
        out_shape=jax.ShapeDtypeStruct((SLOTS, 128), F32),
        compiler_params=params(),
    )(v, pos2)


def final_kernel(v, pos1, state, slot, out, st):
    @pl.when(lax.axis_index("sec") < FLUID_ROWS)
    def _():
        vt = transposed_parts(v[...])

        def one(b, _):
            out[b] = pick(vt, pos1[b], SLOTS)
            return 0

        lax.fori_loop(0, NB, one, 0)

    @pl.when(lax.axis_index("sec") >= FLUID_ROWS)
    def _():
        gather_cells(state[...], st)

        def one(b, _):
            out[b] = cell_values(st, slot[b])
            return 0

        lax.fori_loop(0, NB, one, 0)


def final(v, pos1, state, slot):
    return pl.pallas_call(
        final_kernel,
        out_shape=jax.ShapeDtypeStruct((NB, 1, KB), F32),
        scratch_shapes=[pltpu.VMEM((CX, 2 * CY), BF16)],
        compiler_params=params(),
    )(v, pos1, state, slot)


def over_blk(x):
    return lax.all_to_all(x.reshape(COLS, BROWS, 128), "blk", split_axis=0, concat_axis=0, tiled=True).reshape(SLOTS, 128)


def to_solid(x):
    y = lax.all_gather(x, "sec", axis=0, tiled=True)[:FLUID_ROWS * CROWS]
    return jnp.pad(y, ((0, 8), (0, 0)))


def body(temp, cond, vx, vy, slot, lateral, dest, coef, prior):
    slot, lateral, dest, coef, prior = (v.reshape(NB, 1, KB) for v in (slot, lateral, dest, coef, prior))
    cm, dm, pos1, tb = prep(slot, coef, prior, lateral, dest)
    t_fluid, total, ext = fluid(temp, cond, vx, vy, cm, dm)
    pos2, t2 = compact(over_blk(tb))
    t3 = to_solid(t2)
    counts, lists = make_lists(t3[:2 * ALLP].reshape(ALLP, 256)[:, 0])
    flux = face_flux(total, slot, coef, prior, pos1)
    f3 = to_solid(second(over_blk(flux), pos2))
    source = wall_source(counts, lists, t3, f3)
    t_new = solid_steps(source, t_fluid, ext)
    values = wall_values(counts, lists, t3, t_new[:128])
    reply = jnp.pad(values[:2 * ALLP].reshape(FLUID_ROWS, CROWS, 128), ((0, 2), (0, 0), (0, 0)))
    mine = lax.all_to_all(reply, "sec", split_axis=0, concat_axis=0, tiled=True)[FLUID_ROWS:]
    wall = final(over_blk(back(mine, pos2)), pos1, t_new, slot)
    return t_new, wall.reshape(FACES)


def solution(mesh):
    block, face = P("sec", "blk"), P(("sec", "blk"))
    in_specs = (block, block, block, block, face, P(("sec", "blk"), None), face, face, face)
    return jax.shard_map(body, mesh=mesh, in_specs=in_specs, out_specs=(block, face), check_vma=False)
```

time: 1460 us -> 322 us (0.22)
  the two profiles are of different devices: /device:TPU:15 before, /device:TPU:1 now
where the time goes in v1:
time: 322 us; the launch traced here: 321 us
  Pallas kernels  153 us (48%)
  blocking collectives  140 us (43%)
  starting transfers between devices  14.8 us (5%)
  local copies, waits for them, and re-layouts  7.36 us (2%)
    pallas_call x1, Pallas kernels, fluid(): pl.pallas_call(fluid_kernel, out_shape=[jax.ShapeDtypeStruct((CY, CX), F3...  73.6 us
    all_to_all x1, blocking collectives, body(): lax.all_to_all(reply, 'sec', split_axis=0, concat_axis=0, tiled=True)  69.5 us
    all_gather x2, blocking collectives, to_solid(): y = lax.all_gather(x, 'sec', axis=0, tiled=True)[:FLUID_ROWS * CROWS]  47.1 us
    pallas_call x1, Pallas kernels, prep(): pl.pallas_call(prep_kernel, out_shape=[jax.ShapeDtypeStruct((CY, CX), F32...  25.7 us
    all_to_all x1, blocking collectives, over_blk(): lax.all_to_all(x.reshape(COLS, BROWS, 128), 'blk', split_axis=0, concat_a...  23.7 us
    pallas_call x1, Pallas kernels, face_flux(): pl.pallas_call(flux_kernel, out_shape=jax.ShapeDtypeStruct((SLOTS, 128),...  17.7 us
    all_to_all x2, starting transfers between devices, over_blk(): lax.all_to_all(x.reshape(COLS, BROWS, 128), 'blk', split_axis=0, concat_a...  14.8 us
    pallas_call x1, Pallas kernels, second(): pl.pallas_call(second_kernel, out_shape=jax.ShapeDtypeStruct((CROWS, 128)...  9.16 us
  transfers between devices with their start and end apart: 2, of which 1 were waited for; matrix products, arithmetic and copies ran while one was open for 0% of the time, Pallas kernels for 30%

profile of v1, /device:TPU:1, one launch (start us, length us, event | category | flops | bytes accessed | tf_op | source)
XLA Modules:
  0.0 320.7 jit_solution(15859514894931904530)
XLA Ops:
  0.6 25.7 %shard_map.104 = (f32[256,1024]{1,0:T(8,128)}, f32[256,1024]{1,0:T(8,128)}, s32[16,1,512]{2,1,0:T(1,128)}, s32[128,128]{1,0:T(8,128)}) custom-call(s32[16,1,512]{2,1,0:T(1,128)} %bitcast.14, f32[16,1,512]{2,1,0:T(1,128)} %bitcast.22, f32[16,1,512]{2,1,0:T(1,128)} %bitcast.24, s32[16,1,512]{2,1,0:T(1,128)} %bitcast.27, s32[16,1,512]{2,1,0:T(1,128)} %bitcast.28), custom_call_target="tpu_custom_call" | custom-call | tf_op jit(solution)/shard_map/pallas_call | solution.py:141
  26.3 9.3 %all-to-all-start = ((s32[16,8,128]{2,1,0:T(8,128)}), s32[16,8,128]{2,1,0:T(8,128)S(1)}, u32[]{:S(2)}, u32[]{:S(2)}) async-start(s32[16,8,128]{2,1,0:T(8,128)} %bitcast.26), calls=%async_computation | async-start | bytes 131072 | tf_op jit(solution)/shard_map/all_to_all | solution.py:719
  35.6 73.6 %shard_map.107 = (f32[256,1024]{1,0:T(8,128)}, f32[256,1024]{1,0:T(8,128)}, f32[7,304,1280]{2,1,0:T(8,128)}) custom-call(f32[256,1024]{1,0:T(8,128)} %temp.1, f32[256,1024]{1,0:T(8,128)} %cond.1, f32[256,1024]{1,0:T(8,128)} %vx.1, f32[256,1024]{1,0:T(8,128)} %vy.1, f32[256,1024]{1,0:T(8,128)} %get-tuple-element.17.cm, f32[256,1024]{1,0:T(8,128)} %get-tuple-element.18.dm), custom_call_target="tpu_custom_call" | custom-call | tf_op jit(solution)/shard_map/pallas_call | solution.py:418
  109.3 17.7 %shard_map.108 = f32[128,128]{1,0:T(8,128)} custom-call(f32[256,1024]{1,0:T(8,128)} %get-tuple-element.19.total, s32[16,1,512]{2,1,0:T(1,128)} %bitcast.15, f32[16,1,512]{2,1,0:T(1,128)} %bitcast.23, f32[16,1,512]{2,1,0:T(1,128)} %bitcast.25, s32[16,1,512]{2,1,0:T(1,128)} %get-tuple-element.20.pos1), custom_call_target="tpu_custom_call" | custom-call | tf_op jit(solution)/shard_map/pallas_call | solution.py:468
  127.0 0.0 all-to-all-done
  127.0 0.0 copy-start.2
  127.0 5.5 %all-to-all-start.1 = ((f32[16,8,128]{2,1,0:T(8,128)}), f32[16,8,128]{2,1,0:T(8,128)S(1)}, u32[]{:S(2)}, u32[]{:S(2)}) async-start(f32[16,8,128]{2,1,0:T(8,128)} %bitcast.17), calls=%async_computation.1 | async-start | bytes 131072 | tf_op jit(solution)/shard_map/all_to_all | solution.py:719
  132.5 0.0 copy-done.2
  132.5 5.5 %shard_map.105 = (s32[32,1,512]{2,1,0:T(1,128)}, s32[112,128]{1,0:T(8,128)}) custom-call(s32[128,128]{1,0:T(8,128)} %bitcast.20), custom_call_target="tpu_custom_call" | custom-call | tf_op jit(solution)/shard_map/pallas_call | solution.py:186
  138.0 1.9 all-to-all-done.1
  139.9 0.6 copy-done.1
  140.5 9.2 %shard_map.109 = f32[112,128]{1,0:T(8,128)} custom-call(f32[128,128]{1,0:T(8,128)} %bitcast.18, s32[32,1,512]{2,1,0:T(1,128)} %get-tuple-element.21.pos2), custom_call_target="tpu_custom_call" | custom-call | tf_op jit(solution)/shard_map/pallas_call | solution.py:490
  149.7 23.8 %all_gather.7 = f32[896,128]{1,0:T(8,128)S(1)} all-gather(f32[112,128]{1,0:T(8,128)} %shard_map.109), channel_id=1, replica_groups=mesh['sec'=8,'blk'=16] {'sec'}, dimensions={0}, use_global_device_ids=true | all-gather | bytes 516096 | tf_op jit(solution)/shard_map/all_gather | solution.py:723
  173.5 23.3 %all_gather.6 = s32[896,128]{1,0:T(8,128)S(1)} all-gather(s32[112,128]{1,0:T(8,128)} %get-tuple-element.14), channel_id=1, replica_groups=mesh['sec'=8,'blk'=16] {'sec'}, dimensions={0}, use_global_device_ids=true | all-gather | bytes 516096 | tf_op jit(solution)/shard_map/all_gather | solution.py:723
  196.8 1.6 slice_select_fusion.f
  198.4 0.8 slice_select_fusion.1.t
  199.2 0.0 copy-start
  199.3 0.1 reshape.53
  199.4 0.7 slice_reduce_fusion.first
  200.1 1.3 shard_map.106
  201.4 0.0 copy-done
  201.4 2.1 shard_map.110.source
  203.5 2.5 shard_map.111.state
  206.1 1.9 slice.27.state
  208.0 1.9 shard_map.112
  209.9 1.0 slice.34
  210.9 69.5 %all_to_all.20 = f32[8,112,128]{2,1,0:T(8,128)S(1)} all-to-all(f32[8,112,128]{2,1,0:T(8,128)S(1)} %pad.14), channel_id=1, replica_groups=mesh['sec'=8,'blk'=16] {'sec'}, dimensions={0} | all-to-all | bytes 917504 | tf_op jit(solution)/shard_map/all_to_all | solution.py:740
  280.5 0.7 slice.35.v
  281.1 8.2 %shard_map.113 = f32[128,128]{1,0:T(8,128)} custom-call(f32[2,112,128]{2,1,0:T(8,128)} %slice.35.v, s32[32,1,512]{2,1,0:T(1,128)} %get-tuple-element.21.pos2), custom_call_target="tpu_custom_call" | custom-call | tf_op jit(solution)/shard_map/pallas_call | solution.py:680
  289.3 23.7 %all_to_all.21 = f32[16,8,128]{2,1,0:T(8,128)} all-to-all(f32[16,8,128]{2,1,0:T(8,128)} %bitcast.21), channel_id=1, replica_groups=mesh['sec'=8,'blk'=16] {'blk'}, dimensions={0} | all-to-all | bytes 131072 | tf_op jit(solution)/shard_map/all_to_all | solution.py:719
  313.0 5.4 %shard_map.114 = f32[16,1,512]{2,1,0:T(1,128)} custom-call(f32[128,128]{1,0:T(8,128)} %bitcast.19, s32[16,1,512]{2,1,0:T(1,128)} %get-tuple-element.20.pos1, f32[256,1024]{1,0:T(8,128)} %shard_map.111.state, s32[16,1,512]{2,1,0:T(1,128)} %bitcast.16), custom_call_target="tpu_custom_call" | custom-call | tf_op jit(solution)/shard_map/pallas_call | solution.py:710
  318.4 2.3 copy.15
  (3 shorter events, 0.1 us)
Async XLA Ops:
  26.3 100.6 %all-to-all-start = ((s32[16,8,128]{2,1,0:T(8,128)}), s32[16,8,128]{2,1,0:T(8,128)S(1)}, u32[]{:S(2)}, u32[]{:S(2)}) async-start(s32[16,8,128]{2,1,0:T(8,128)} %bitcast.26), calls=%async_computation | async-start | bytes 131072 | tf_op jit(solution)/shard_map/all_to_all | solution.py:719
  127.0 5.5 %copy-start.2 = (s32[16,8,128]{2,1,0:T(8,128)}, s32[16,8,128]{2,1,0:T(8,128)S(1)}, u32[]{:S(2)}) copy-start(s32[16,8,128]{2,1,0:T(8,128)S(1)} %all-to-all-done) | copy-start | bytes 196612
  127.0 12.9 %all-to-all-start.1 = ((f32[16,8,128]{2,1,0:T(8,128)}), f32[16,8,128]{2,1,0:T(8,128)S(1)}, u32[]{:S(2)}, u32[]{:S(2)}) async-start(f32[16,8,128]{2,1,0:T(8,128)} %bitcast.17), calls=%async_computation.1 | async-start | bytes 131072 | tf_op jit(solution)/shard_map/all_to_all | solution.py:719
  139.9 0.6 copy-start.1
  199.2 2.2 copy-start

commit v2 on v0

v2 whole, which is shorter than its diff:
```python
import functools

import jax
import jax.numpy as jnp
from jax import lax
from jax.experimental import pallas as pl
from jax.experimental.pallas import tpu as pltpu
from jax.sharding import PartitionSpec as P

F32, BF16, I32 = jnp.float32, jnp.bfloat16, jnp.int32
MESH = pl.DeviceIdType.MESH
NT = (((1,), (1,)), ((), ()))

CY, CX = 256, 1024
FACES = 8192
FLUID_ROWS, SECS, COLS = 6, 8, 16
FLUID_STEPS, SOLID_STEPS = 10, 4
DT = 0.2
FROWS = FACES // 128
KR = 512
HALO = 16
BROWS = 8
SLOTS = COLS * BROWS
PAIRS = 56
CROWS = 2 * PAIRS
ALLP = FLUID_ROWS * PAIRS
QUAD = 4
LROWS = 4
HY, OY, TILES = 304, 24, 9
VLIM = 60 << 20


def params(**kw):
    return pltpu.CompilerParams(vmem_limit_bytes=VLIM, **kw)


def iota(shape, dim):
    return lax.broadcasted_iota(I32, shape, dim)


def split2(x):
    hi = x.astype(BF16).astype(F32)
    return hi, (x - hi).astype(BF16).astype(F32)


def onehot(mask):
    return jnp.where(mask, 1.0, 0.0).astype(BF16)


def dot(a, b):
    return jnp.dot(a, b, preferred_element_type=F32)


def dot_nt(a, b):
    return lax.dot_general(a, b, NT, preferred_element_type=F32)


def lane_row(ref, b, n):
    return jnp.concatenate([ref[pl.ds(n * b + i, 1), :] for i in range(n)], axis=1)


def put_lane_row(ref, b, n, v):
    for i in range(n):
        ref[pl.ds(n * b + i, 1), :] = v[:, i * 128:(i + 1) * 128]


def ranks(group, nb, ng, o_ref, p_ref):
    for b in range(nb):
        o_ref[b * ng:(b + 1) * ng, :] = jnp.where(iota((ng, KR), 0) == group(b), 1.0, 0.0)
    o = o_ref[...].astype(BF16)
    p_ref[...] = dot(o, onehot(iota((KR, KR), 0) < iota((KR, KR), 1)))
    return dot(o, onehot(iota((KR, 128), 0) >= 0))


def ranked(b, ng, carry, o_ref, p_ref):
    rows = slice(b * ng, (b + 1) * ng)
    place = p_ref[rows] + jnp.concatenate([carry] * (KR // 128), axis=1)
    return jnp.sum(o_ref[rows] * place, axis=0, keepdims=True).astype(I32)


def spread_rows(pos, pieces, rows):
    k = pos.shape[1]
    hit = iota((rows, k), 0) == (pos >> 7)
    a = jnp.concatenate([jnp.where(hit, v, 0.0).astype(BF16) for v in pieces], axis=0)
    return dot_nt(a, onehot(iota((128, k), 0) == (pos & 127)))


def spread_all(pos, parts_of, n_parts, rows, total_rows, out):
    out[...] = jnp.zeros_like(out)

    def one(b, _):
        out[...] += spread_rows(lane_row(pos, b, 16), parts_of(b), rows)
        return 0

    lax.fori_loop(0, total_rows // 16, one, 0)


def pick(vt, pos, rows):
    k = pos.shape[1]
    r = onehot(iota((rows, k), 0) == (pos >> 7))
    g = dot(vt, jnp.concatenate([r, r], axis=0))
    return jnp.sum(jnp.where(iota((128, k), 0) == (pos & 127), g, 0.0), axis=0, keepdims=True)


def pick_all(vt, pos, rows, total_rows, out):
    def one(b, _):
        put_lane_row(out, b, 16, pick(vt, lane_row(pos, b, 16), rows))
        return 0

    lax.fori_loop(0, total_rows // 16, one, 0)


def transposed_parts(v):
    hi, lo = split2(v.T)
    return jnp.concatenate([hi, lo], axis=1).astype(BF16)


def target_parts(t):
    return (t >> 10).astype(F32), ((t >> 5) & 31).astype(F32), (t & 31).astype(F32)


def target_join(x, rows):
    return (x[0:rows] * 1024.0 + x[rows:2 * rows] * 32.0 + x[2 * rows:3 * rows]).astype(I32)


def gather_cells(tile_of, st):
    for j in range(CX // 128):
        hi, lo = split2(tile_of(j).T)
        st[128 * j:128 * j + 128, 0:CY] = hi.astype(BF16)
        st[128 * j:128 * j + 128, CY:2 * CY] = lo.astype(BF16)


def cell_values(st, s):
    k = s.shape[1]
    r = onehot(iota((CY, k), 0) == (s >> 10))
    g = dot(st[...], jnp.concatenate([r, r], axis=0))
    tile = (s & 1023) >> 7
    a = g[0:128]
    for i in range(1, CX // 128):
        a = jnp.where(tile == i, g[128 * i:128 * i + 128], a)
    return jnp.sum(jnp.where(iota((128, k), 0) == (s & 127), a, 0.0), axis=0, keepdims=True)


def signal(to):
    pl.semaphore_signal(pltpu.get_barrier_semaphore(), inc=1, device_id=to, device_id_type=MESH)


def arrive(ref, sem):
    pltpu.make_async_copy(ref, ref, sem).wait()


def push(src, dst, send, recv, to):
    copy = pltpu.make_async_remote_copy(src, dst, send, recv, device_id=to, device_id_type=MESH)
    copy.start()
    return copy


def exchange(src, land, send, recv, sec, blk):
    def one(q, _):
        @pl.when(q != blk)
        def _():
            push(src.at[pl.ds(pl.multiple_of(q * BROWS, 8), BROWS)], land.at[pl.ds(pl.multiple_of(blk * BROWS, 8), BROWS)],
                 send, recv, (sec, q))
        return 0

    lax.fori_loop(0, COLS, one, 0)
    own = pl.ds(pl.multiple_of(blk * BROWS, 8), BROWS)
    land[own, :] = src[own, :]
    arrive(src.at[pl.ds(0, SLOTS - BROWS)], send)
    arrive(land.at[pl.ds(0, SLOTS - BROWS)], recv)


def greet_peers(sec, blk):
    def one(q, _):
        @pl.when(q != blk)
        def _():
            signal((sec, q))
        return 0

    lax.fori_loop(0, COLS, one, 0)


def lane_roll(x, n):
    return pltpu.roll(x, n % 128, 1)


def beside(x):
    lane = iota((8, 128), 1)
    east, west = [lane_roll(v, 127) for v in x], [lane_roll(v, 1) for v in x]
    e = [jnp.where(lane == 127, east[(j + 1) % TILES], east[j]) for j in range(TILES)]
    w = [jnp.where(lane == 0, west[j - 1], west[j]) for j in range(TILES)]
    return e, w


def advance(src, dst, c, total, r):
    rows = pl.ds(r, 8)
    x = [src[j, rows, :] for j in range(TILES)]
    e, w = beside(x)
    for j in range(TILES):
        n, s = src[j, pl.ds(r + 1, 8), :], src[j, pl.ds(r - 1, 8), :]
        if total is not None and j < TILES - 1:
            total[j, rows, :] += x[j]
        dst[j, rows, :] = (
            (c[4, j, rows, :] * x[j] + c[0, j, rows, :] * n)
            + (c[1, j, rows, :] * s + c[2, j, rows, :] * e[j])
            + (c[3, j, rows, :] * w[j] + c[5, j, rows, :])
        )


def strips(fn, first, count, unroll):
    def body(i, _):
        for u in range(unroll):
            fn(pl.multiple_of(8 * first + 8 * unroll * i + 8 * u, 8))
        return 0

    lax.fori_loop(0, count // unroll, body, 0)


def substeps(a, b, c, total, count):
    def two(i, _):
        strips(lambda r: advance(a, b, c, total, r), 1, 36, 6)
        strips(lambda r: advance(b, a, c, total, r), 1, 36, 6)
        return 0

    lax.fori_loop(0, count // 2, two, 0)


def coefficients(e, c, low, high, r):
    rows = pl.ds(r, 8)
    x = [e[1, j, rows, :] for j in range(TILES)]
    east, west = beside(x)
    at = r + iota((8, 128), 0)
    first, last = low & (at == OY), high & (at == OY + CY - 1)
    h = 0.5 * DT
    for j in range(TILES):
        hn, hs = h * (x[j] + e[1, j, pl.ds(r + 1, 8), :]), h * (x[j] + e[1, j, pl.ds(r - 1, 8), :])
        he, hw = h * (x[j] + east[j]), h * (x[j] + west[j])
        vx, vy = h * e[2, j, rows, :], h * e[3, j, rows, :]
        an, as_ = hn - vy, hs + vy
        c0 = 1.0 - ((hn + hs) + (he + hw)) - DT * e[4, j, rows, :]
        c[0, j, rows, :] = jnp.where(last, 0.0, an)
        c[1, j, rows, :] = jnp.where(first, 0.0, as_)
        c[2, j, rows, :] = he - vx
        c[3, j, rows, :] = hw + vx
        c[4, j, rows, :] = c0 + jnp.where(first, as_, 0.0) + jnp.where(last, an, 0.0)
        c[5, j, rows, :] = DT * e[5, j, rows, :]


def compact(t, pos, t2, o_ref, p_ref, out):
    nb, ng = SLOTS // 4, 8

    def group(b):
        v = lane_row(t, b, 4)
        return jnp.where(v >= 1024, ((v - 1024) >> 17) * 4 + ((v >> 8) & 3), -1)

    totals = ranks(group, nb, ng, o_ref, p_ref)
    count = jnp.zeros((ng, 128), F32)
    for b in range(nb):
        count = count + totals[b * ng:(b + 1) * ng]
    units = ((count.astype(I32) + 255) >> 8).astype(F32).astype(BF16)
    carry = dot(onehot(iota((ng, ng), 1) < iota((ng, ng), 0)), units) * 256.0
    for b in range(nb):
        put_lane_row(pos, b, 4, jnp.where(lane_row(t, b, 4) >= 1024, ranked(b, ng, carry, o_ref, p_ref), -1))
        carry = carry + totals[b * ng:(b + 1) * ng]
    spread_all(pos, lambda b: target_parts(lane_row(t, b, 16)), 3, CROWS, SLOTS, out)
    t2[...] = target_join(out[...], CROWS)


def fluid_kernel(temp, cond, vx, vy, slot, coef, prior, lateral, dest,
                 t_out, s_out, ext, pos1, pos2, t3,
                 e, t_b, c, total, acc, pack, land, packm, landm, tb, tb_land, p2, p2_land, t2, o_ref, p_ref, tb_out, t2_out,
                 send, recv, face_send, face_recv, local):
    sec, blk = lax.axis_index("sec"), lax.axis_index("blk")
    fluid = sec < FLUID_ROWS
    solid = jnp.logical_not(fluid)
    low = (sec == 0) | (sec == FLUID_ROWS)
    high = (sec == FLUID_ROWS - 1) | (sec == SECS - 1)
    has_low, has_high = jnp.logical_not(low), jnp.logical_not(high)
    left, right = lax.rem(blk + COLS - 1, COLS), lax.rem(blk + 1, COLS)
    server = FLUID_ROWS + sec // 3
    mine = 3 * (sec - FLUID_ROWS)
    other = 2 * FLUID_ROWS + 1 - sec

    signal((sec, left))
    signal((sec, right))

    @pl.when(has_low)
    def _():
        signal((sec - 1, blk))

    @pl.when(has_high)
    def _():
        signal((sec + 1, blk))

    @pl.when(fluid)
    def _():
        signal((server, blk))

    @pl.when(solid)
    def _():
        def one(i, _):
            signal((mine + i // COLS, lax.rem(i, COLS)))
            return 0

        lax.fori_loop(0, 3 * COLS, one, 0)

    mid = slice(OY, OY + CY)
    keep = jnp.where(fluid, 1.0, 0.0)
    for j in range(TILES - 1):
        tile = slice(128 * j, 128 * j + 128)
        e[0, j, mid, :] = temp[:, tile]
        e[1, j, mid, :] = cond[:, tile]
        e[2, j, mid, :] = vx[:, tile] * keep
        e[3, j, mid, :] = vy[:, tile] * keep

    @pl.when(low)
    def _():
        for a in range(6):
            for j in range(TILES - 1):
                e[a, j, OY - HALO:OY, :] = jnp.zeros((HALO, 128), F32)

    @pl.when(high)
    def _():
        for a in range(6):
            for j in range(TILES - 1):
                e[a, j, OY + CY:OY + CY + HALO, :] = jnp.zeros((HALO, 128), F32)

    pl.semaphore_wait(
        pltpu.get_barrier_semaphore(),
        4 - low.astype(I32) - high.astype(I32) + jnp.where(fluid, COLS, 3))

    def rows_copy(first, arrays, src, dst, i, to):
        return pltpu.make_async_remote_copy(
            e.at[pl.ds(first, arrays), pl.ds(0, TILES - 1), pl.ds(src, HALO)],
            e.at[pl.ds(first, arrays), pl.ds(0, TILES - 1), pl.ds(dst, HALO)],
            send.at[i], recv.at[i], device_id=to, device_id_type=MESH)

    def rows_pair(first, arrays, i):
        return (rows_copy(first, arrays, OY, OY + CY, i, (sec - 1, blk)),
                rows_copy(first, arrays, OY + CY - HALO, OY - HALO, i + 1, (sec + 1, blk)))

    def rows_start(pair):
        pl.when(has_low)(pair[0].start)
        pl.when(has_high)(pair[1].start)

    def rows_wait(pair):
        @pl.when(has_low)
        def _():
            pair[0].wait_send()
            pair[1].wait_recv()

        @pl.when(has_high)
        def _():
            pair[1].wait_send()
            pair[0].wait_recv()

    def cols_start(first, arrays, i, pack, land):
        lane = iota((8, 128), 1)

        def strip(r):
            rows = pl.ds(r, 8)
            lo = e[first, 0, rows, :]
            hi = lane_roll(e[first, TILES - 2, rows, :], HALO)
            for a in range(1, arrays):
                here = (lane >> 4) == a
                lo = jnp.where(here, lane_roll(e[first + a, 0, rows, :], HALO * a), lo)
                hi = jnp.where(here, lane_roll(e[first + a, TILES - 2, rows, :], HALO * a + HALO), hi)
            pack[0, rows, :] = lo
            pack[1, rows, :] = hi

        strips(strip, 1, 36, 4)
        return (push(pack.at[0, pl.ds(8, 288)], land.at[0, pl.ds(8, 288)], send.at[i], recv.at[i], (sec, left)),
                push(pack.at[1, pl.ds(8, 288)], land.at[1, pl.ds(8, 288)], send.at[i + 1], recv.at[i + 1], (sec, right)))

    def cols_wait(pair, first, arrays, land):
        pair[0].wait()
        pair[1].wait()
        lane = iota((8, 128), 1)

        def strip(r):
            rows = pl.ds(r, 8)
            lo, hi = land[0, rows, :], land[1, rows, :]
            for a in range(arrays):
                e[first + a, TILES - 1, rows, :] = jnp.where(
                    lane < 64, lane_roll(lo, -HALO * a), lane_roll(hi, 128 - HALO - HALO * a))

        strips(strip, 1, 36, 4)

    static_rows = rows_pair(0, 4, 0)
    rows_start(static_rows)

    acc[...] = jnp.zeros_like(acc)

    def maps(b, _):
        s, k = lane_row(slot, b, 8), lane_row(coef, b, 8)
        parts = split2(k) + split2(k * lane_row(prior, b, 8))
        hit = iota((CY, 1024), 0) == (s >> 10)
        a = jnp.concatenate([jnp.where(hit, v, 0.0).astype(BF16) for v in parts], axis=0)
        acc[...] += dot_nt(a, onehot(iota((CX, 1024), 0) == (s & 1023)))
        return 0

    lax.fori_loop(0, 4, maps, 0)
    rows_wait(static_rows)
    static_cols = cols_start(0, 4, 2, pack, land)
    lax.fori_loop(4, 8, maps, 0)
    for j in range(TILES - 1):
        tile = slice(128 * j, 128 * j + 128)
        e[4, j, mid, :] = acc[0:CY, tile] + acc[CY:2 * CY, tile]
        e[5, j, mid, :] = acc[2 * CY:3 * CY, tile] + acc[3 * CY:4 * CY, tile]
    map_rows = rows_pair(4, 2, 4)
    rows_start(map_rows)
    cols_wait(static_cols, 0, 4, land)

    totals = ranks(lambda b: lane_row(lateral, b, 4), FROWS // 4, COLS, o_ref, p_ref)
    carry = jnp.zeros((COLS, 128), F32)
    for b in range(FROWS // 4):
        put_lane_row(pos1, b, 4, lane_row(lateral, b, 4) * (BROWS * 128) + ranked(b, COLS, carry, o_ref, p_ref))
        carry = carry + totals[b * COLS:(b + 1) * COLS]

    rows_wait(map_rows)
    map_cols = cols_start(4, 2, 6, packm, landm)
    spread_all(pos1, lambda b: target_parts(lane_row(dest, b, 16) + 1024), 3, SLOTS, FROWS, tb_out)

    @pl.when(fluid)
    def _():
        tb[...] = target_join(tb_out[...], SLOTS)

        def one(q, _):
            push(tb.at[pl.ds(pl.multiple_of(q * BROWS, 8), BROWS)],
                 tb_land.at[pl.ds(pl.multiple_of(lax.rem(sec, 3) * SLOTS + blk * BROWS, 8), BROWS)],
                 face_send.at[0], face_recv.at[0], (server, q))
            return 0

        lax.fori_loop(0, COLS, one, 0)

    cols_wait(map_cols, 4, 2, landm)
    strips(lambda r: coefficients(e, c, low, high, r), 1, 36, 4)

    @pl.when(fluid)
    def _():
        total[...] = jnp.zeros_like(total)
        substeps(e.at[0], t_b, c, total, FLUID_STEPS)
        for j in range(TILES - 1):
            t_out[:, 128 * j:128 * j + 128] = e[0, j, mid, :]
            s_out[j] = total[j, mid, :]
        arrive(tb, face_send.at[0])
        arrive(p2_land, face_recv.at[1])
        pos2[...] = p2_land[...]
        t3[...] = jnp.zeros_like(t3)

    @pl.when(solid)
    def _():
        first = pltpu.make_async_copy(e.at[0], ext.at[0], local.at[0])
        rest = pltpu.make_async_copy(c, ext.at[pl.ds(1, 6)], local.at[1])
        first.start()
        rest.start()
        t_out[...] = jnp.zeros_like(t_out)
        s_out[...] = jnp.zeros_like(s_out)
        pos2[...] = jnp.zeros_like(pos2)
        arrive(tb_land, face_recv.at[0])
        for i in range(3):
            t = tb_land.at[pl.ds(i * SLOTS, SLOTS)]
            compact(t, p2.at[i], t2.at[0, pl.ds(i * CROWS, CROWS)], o_ref, p_ref, t2_out)
            push(p2.at[i], p2_land, face_send.at[1], face_recv.at[1], (mine + i, blk))
        swap = push(t2.at[0], t2.at[1], face_send.at[2], face_recv.at[2], (other, blk))
        arrive(p2, face_send.at[1])
        swap.wait()
        half = 3 * CROWS

        @pl.when(sec == FLUID_ROWS)
        def _():
            t3[0:half] = t2[0]
            t3[half:2 * half] = t2[1]

        @pl.when(sec == SECS - 1)
        def _():
            t3[0:half] = t2[1]
            t3[half:2 * half] = t2[0]

        t3[2 * half:] = jnp.zeros((8, 128), I32)
        first.wait()
        rest.wait()


def fluid(temp, cond, vx, vy, slot, coef, prior, lateral, dest):
    vm = pl.BlockSpec(memory_space=pltpu.VMEM)
    return pl.pallas_call(
        fluid_kernel,
        out_shape=[
            jax.ShapeDtypeStruct((CY, CX), F32), jax.ShapeDtypeStruct((TILES - 1, CY, 128), F32),
            jax.ShapeDtypeStruct((7, TILES, HY, 128), F32),
            jax.ShapeDtypeStruct((FROWS, 128), I32), jax.ShapeDtypeStruct((SLOTS, 128), I32),
            jax.ShapeDtypeStruct((2 * ALLP + 8, 128), I32),
        ],
        in_specs=[vm] * 9,
        out_specs=[vm, vm, pl.BlockSpec(memory_space=pl.ANY), vm, vm, vm],
        scratch_shapes=[
            pltpu.VMEM((6, TILES, HY, 128), F32), pltpu.VMEM((TILES, HY, 128), F32), pltpu.VMEM((6, TILES, HY, 128), F32),
            pltpu.VMEM((TILES - 1, HY, 128), F32), pltpu.VMEM((4 * CY, CX), F32),
            pltpu.VMEM((2, HY, 128), F32), pltpu.VMEM((2, HY, 128), F32),
            pltpu.VMEM((2, HY, 128), F32), pltpu.VMEM((2, HY, 128), F32),
            pltpu.VMEM((SLOTS, 128), I32), pltpu.VMEM((3 * SLOTS, 128), I32),
            pltpu.VMEM((3, SLOTS, 128), I32), pltpu.VMEM((SLOTS, 128), I32), pltpu.VMEM((2, 3 * CROWS, 128), I32),
            pltpu.VMEM((256, KR), F32), pltpu.VMEM((256, KR), F32),
            pltpu.VMEM((3 * SLOTS, 128), F32), pltpu.VMEM((3 * CROWS, 128), F32),
            pltpu.SemaphoreType.DMA((8,)), pltpu.SemaphoreType.DMA((8,)),
            pltpu.SemaphoreType.DMA((3,)), pltpu.SemaphoreType.DMA((3,)), pltpu.SemaphoreType.DMA((2,)),
        ],
        compiler_params=params(collective_id=0, has_side_effects=True),
    )(temp, cond, vx, vy, slot, coef, prior, lateral, dest)


def list_kernel(t, counts, lists):
    sec = lax.axis_index("sec")

    @pl.when(sec < FLUID_ROWS)
    def _():
        counts[...] = jnp.zeros_like(counts)
        lists[...] = jnp.zeros_like(lists)

    @pl.when(sec >= FLUID_ROWS)
    def _():
        n = 768
        v = jnp.concatenate([t[...].T[0:8], jnp.zeros((8, n - 2 * ALLP - 8), I32)], axis=1)[0:1]
        row = iota((1, n), 1)
        ours = (v >= 1024) & (((v - 1024) >> 17) == sec - FLUID_ROWS) & ((row & 1) == 0)
        group = jnp.where(ours, (v >> 8) & 3, -1)
        member = jnp.where(iota((8, n), 0) == group, 1.0, 0.0)
        before = dot(member.astype(BF16), onehot(iota((n, n), 0) < iota((n, n), 1)))
        rank = jnp.sum(member * before, axis=0, keepdims=True).astype(I32)
        pos = jnp.where(ours, group * (LROWS * 128) + rank, -1)
        back = (row >> 1) - ALLP
        x = spread_rows(pos, ((back >> 1).astype(F32), (back & 1).astype(F32)), 4 * LROWS)
        lists[...] = (2.0 * x[0:4 * LROWS] + x[4 * LROWS:]).astype(I32) + ALLP
        counts[...] = dot(member.astype(BF16), onehot(iota((n, 128), 0) >= 0)).astype(I32)


def make_lists(t):
    return pl.pallas_call(
        list_kernel,
        out_shape=[jax.ShapeDtypeStruct((8, 128), I32), jax.ShapeDtypeStruct((4 * LROWS, 128), I32)],
        compiler_params=params(),
    )(t)


def listed(lists, g, n):
    return lists[g * LROWS + (n >> 7), n & 127]


def pair_row(ref, lists, g, i):
    rows = []
    for j in range(QUAD):
        p = listed(lists, g, QUAD * i + j)
        rows += [ref[pl.ds(2 * p, 1), :], ref[pl.ds(2 * p + 1, 1), :]]
    return jnp.concatenate(rows, axis=1)


def flux_kernel(total, slot, coef, prior, pos1, pos2, counts, f3, st, fb, land, f2, f3_land, spread, send, recv):
    sec, blk = lax.axis_index("sec"), lax.axis_index("blk")

    @pl.when(sec < FLUID_ROWS)
    def _():
        greet_peers(sec, blk)
        gather_cells(lambda j: total[j], st)
        spread[...] = jnp.zeros_like(spread)

        def one(b, _):
            value = cell_values(st, lane_row(slot, b, 8)) * (1.0 / FLUID_STEPS)
            flux = lane_row(coef, b, 8) * (value - lane_row(prior, b, 8))
            spread[...] += spread_rows(lane_row(pos1, b, 8), split2(flux), SLOTS)
            return 0

        lax.fori_loop(0, FROWS // 8, one, 0)
        fb[...] = spread[0:SLOTS] + spread[SLOTS:2 * SLOTS]
        pl.semaphore_wait(pltpu.get_barrier_semaphore(), COLS + 1)
        exchange(fb, land, send.at[0], recv.at[0], sec, blk)
        part = spread.at[pl.ds(0, 2 * CROWS)]
        spread_all(pos2, lambda b: split2(lane_row(land, b, 16)), 2, CROWS, SLOTS, part)
        f2[...] = part[0:CROWS] + part[CROWS:2 * CROWS]
        place = f3_land.at[pl.ds(pl.multiple_of(sec * CROWS, 8), CROWS)]
        a = push(f2, place, send.at[1], recv.at[1], (FLUID_ROWS, blk))
        b = push(f2, place, send.at[2], recv.at[1], (SECS - 1, blk))
        f3[...] = jnp.zeros_like(f3)
        a.wait_send()
        b.wait_send()

    @pl.when(sec >= FLUID_ROWS)
    def _():
        for r in range(FLUID_ROWS):
            signal((r, blk))
        arrive(f3_land, recv.at[1])
        f3[0:2 * ALLP] = f3_land[...]
        f3[2 * ALLP:] = jnp.zeros((8, 128), F32)


def face_flux(total, slot, coef, prior, pos1, pos2, counts):
    return pl.pallas_call(
        flux_kernel,
        out_shape=jax.ShapeDtypeStruct((2 * ALLP + 8, 128), F32),
        in_specs=[pl.BlockSpec(memory_space=pltpu.VMEM)] * 6 + [pl.BlockSpec(memory_space=pl.ANY)],
        scratch_shapes=[
            pltpu.VMEM((CX, 2 * CY), BF16), pltpu.VMEM((SLOTS, 128), F32), pltpu.VMEM((SLOTS, 128), F32),
            pltpu.VMEM((CROWS, 128), F32), pltpu.VMEM((2 * ALLP, 128), F32), pltpu.VMEM((2 * SLOTS, 128), F32),
            pltpu.SemaphoreType.DMA((3,)), pltpu.SemaphoreType.DMA((2,)),
        ],
        compiler_params=params(collective_id=1, has_side_effects=True),
    )(total, slot, coef, prior, pos1, pos2, counts)


def source_kernel(counts, lists, t, f, out, acc):
    sec = lax.axis_index("sec")

    @pl.when(sec >= FLUID_ROWS)
    def _():
        base = 128 * (sec - FLUID_ROWS) + 1
        n = QUAD * 256
        for g in range(4):
            acc[...] = jnp.zeros_like(acc)

            def one(i, _):
                v = pair_row(t, lists, g, i)
                hi, lo = split2(pair_row(f, lists, g, i))
                hit = iota((128, n), 0) == (v >> 10) - base
                a = jnp.concatenate([jnp.where(hit, p, 0.0).astype(BF16) for p in (hi, lo)], axis=0)
                acc[...] += dot_nt(a, onehot(iota((256, n), 0) == (v & 255)))
                return 0

            lax.fori_loop(0, (counts[g, 0] + QUAD - 1) // QUAD, one, 0)
            out[:, 256 * g:256 * (g + 1)] = acc[0:128] + acc[128:256]

    @pl.when(sec < FLUID_ROWS)
    def _():
        out[...] = jnp.zeros_like(out)


def wall_source(counts, lists, t, f):
    return pl.pallas_call(
        source_kernel,
        in_specs=[pl.BlockSpec(memory_space=pltpu.SMEM)] * 2 + [pl.BlockSpec(memory_space=pltpu.VMEM)] * 2,
        out_shape=jax.ShapeDtypeStruct((128, CX), F32),
        scratch_shapes=[pltpu.VMEM((256, 256), F32)],
        compiler_params=params(),
    )(counts, lists, t, f)


def wall_kernel(counts, lists, t, state, out, t_out):
    sec = lax.axis_index("sec")
    out[...] = jnp.zeros_like(out)
    t_out[...] = state[...]

    @pl.when(sec >= FLUID_ROWS)
    def _():
        base = 128 * (sec - FLUID_ROWS) + 1
        n = QUAD * 256
        for g in range(4):
            table = transposed_parts(state[0:128, 256 * g:256 * (g + 1)])

            def one(i, _):
                v = pair_row(t, lists, g, i)
                r = onehot(iota((128, n), 0) == (v >> 10) - base)
                x = dot(table, jnp.concatenate([r, r], axis=0))
                x = jnp.where(((v >> 7) & 1) == 1, x[128:256], x[0:128])
                x = jnp.sum(jnp.where(iota((128, n), 0) == (v & 127), x, 0.0), axis=0, keepdims=True)
                for j in range(QUAD):
                    p = listed(lists, g, QUAD * i + j)
                    out[pl.ds(2 * p, 1), :] = x[:, 256 * j:256 * j + 128]
                    out[pl.ds(2 * p + 1, 1), :] = x[:, 256 * j + 128:256 * j + 256]
                return 0

            lax.fori_loop(0, (counts[g, 0] + QUAD - 1) // QUAD, one, 0)


def wall_values(counts, lists, t, state):
    return pl.pallas_call(
        wall_kernel,
        in_specs=[pl.BlockSpec(memory_space=pltpu.SMEM)] * 2 + [pl.BlockSpec(memory_space=pltpu.VMEM)] * 2,
        out_shape=[jax.ShapeDtypeStruct((2 * ALLP + 8, 128), F32), jax.ShapeDtypeStruct((CY, CX), F32)],
        compiler_params=params(),
    )(counts, lists, t, state)


def solid_kernel(source, t_fluid, ext, t_out, e, c, x, pack, land, send, recv, local):
    sec, blk = lax.axis_index("sec"), lax.axis_index("blk")
    mid = slice(OY, OY + CY)

    @pl.when(sec < FLUID_ROWS)
    def _():
        t_out[...] = t_fluid[...]

    @pl.when(sec >= FLUID_ROWS)
    def _():
        left, right = lax.rem(blk + COLS - 1, COLS), lax.rem(blk + 1, COLS)
        other = 2 * FLUID_ROWS + 1 - sec
        for to in ((sec, left), (sec, right), (other, blk)):
            signal(to)
        first = pltpu.make_async_copy(ext.at[0], e.at[0], local.at[0])
        rest = pltpu.make_async_copy(ext.at[pl.ds(1, 6)], c, local.at[1])
        first.start()
        rest.start()
        for j in range(TILES):
            x[j, 0:OY] = jnp.zeros((OY, 128), F32)
            x[j, OY + 128:OY + CY] = jnp.zeros((CY - 128, 128), F32)
        for j in range(TILES - 1):
            x[j, OY:OY + 128] = DT * source[:, 128 * j:128 * j + 128]

        @pl.when(sec == SECS - 1)
        def _():
            for j in range(TILES):
                x[j, OY + CY:] = jnp.zeros((HY - OY - CY, 128), F32)

        pl.semaphore_wait(pltpu.get_barrier_semaphore(), 3)
        up = pltpu.make_async_remote_copy(
            x.at[pl.ds(0, TILES - 1), pl.ds(OY, HALO)], x.at[pl.ds(0, TILES - 1), pl.ds(OY + CY, HALO)],
            send.at[2], recv.at[2], device_id=(other, blk), device_id_type=MESH)

        @pl.when(sec == SECS - 1)
        def _():
            up.start()
            up.wait_send()

        @pl.when(sec == FLUID_ROWS)
        def _():
            up.wait_recv()

        parts = ((0, OY, 128), (128, OY + CY, HALO))
        for at, fro, size in parts:
            pack[0, at:at + size] = x[0, fro:fro + size]
            pack[1, at:at + size] = x[TILES - 2, fro:fro + size]
        to_left = push(pack.at[0], land.at[0], send.at[0], recv.at[0], (sec, left))
        to_right = push(pack.at[1], land.at[1], send.at[1], recv.at[1], (sec, right))
        to_left.wait()
        to_right.wait()
        for at, fro, size in parts:
            x[TILES - 1, fro:fro + size] = jnp.where(iota((size, 128), 1) < 64, land[0, at:at + size], land[1, at:at + size])
        first.wait()
        rest.wait()

        def drive(r):
            rows = pl.ds(r, 8)
            for j in range(TILES):
                c[5, j, rows, :] += x[j, rows, :]

        strips(drive, 2, 34, 2)
        substeps(e.at[0], e.at[1], c, None, SOLID_STEPS)
        for j in range(TILES - 1):
            t_out[:, 128 * j:128 * j + 128] = e[0, j, mid, :]


def solid_steps(source, t_fluid, ext):
    vm = pl.BlockSpec(memory_space=pltpu.VMEM)
    return pl.pallas_call(
        solid_kernel,
        out_shape=jax.ShapeDtypeStruct((CY, CX), F32),
        in_specs=[vm, vm, pl.BlockSpec(memory_space=pl.ANY)],
        out_specs=vm,
        scratch_shapes=[
            pltpu.VMEM((2, TILES, HY, 128), F32), pltpu.VMEM((6, TILES, HY, 128), F32), pltpu.VMEM((TILES, HY, 128), F32),
            pltpu.VMEM((2, 144, 128), F32), pltpu.VMEM((2, 144, 128), F32),
            pltpu.SemaphoreType.DMA((3,)), pltpu.SemaphoreType.DMA((3,)), pltpu.SemaphoreType.DMA((2,)),
        ],
        compiler_params=params(collective_id=2, has_side_effects=True),
    )(source, t_fluid, ext)


def back_kernel(values, pos1, pos2, state, slot, out, reply, fb, land, st, send, recv):
    sec, blk = lax.axis_index("sec"), lax.axis_index("blk")

    @pl.when(sec < FLUID_ROWS)
    def _():
        greet_peers(sec, blk)
        signal((FLUID_ROWS, blk))
        signal((SECS - 1, blk))
        pl.semaphore_wait(pltpu.get_barrier_semaphore(), COLS - 1)
        arrive(reply, recv.at[0])
        pick_all(transposed_parts(reply[0] + reply[1]), pos2, CROWS, SLOTS, fb)
        exchange(fb, land, send.at[1], recv.at[1], sec, blk)
        pick_all(transposed_parts(land[...]), pos1, SLOTS, FROWS, out)

    @pl.when(sec >= FLUID_ROWS)
    def _():
        pl.semaphore_wait(pltpu.get_barrier_semaphore(), FLUID_ROWS)
        for r in range(FLUID_ROWS):
            push(values.at[pl.ds(r * CROWS, CROWS)], reply.at[sec - FLUID_ROWS], send.at[0], recv.at[0], (r, blk))
        gather_cells(lambda j: state[:, 128 * j:128 * j + 128], st)

        def one(b, _):
            put_lane_row(out, b, 8, cell_values(st, lane_row(slot, b, 8)))
            return 0

        lax.fori_loop(0, FROWS // 8, one, 0)
        arrive(values.at[pl.ds(0, 2 * ALLP)], send.at[0])


def back(values, pos1, pos2, state, slot):
    return pl.pallas_call(
        back_kernel,
        out_shape=jax.ShapeDtypeStruct((FROWS, 128), F32),
        in_specs=[pl.BlockSpec(memory_space=pltpu.VMEM)] * 5,
        scratch_shapes=[
            pltpu.VMEM((2, CROWS, 128), F32), pltpu.VMEM((SLOTS, 128), F32), pltpu.VMEM((SLOTS, 128), F32),
            pltpu.VMEM((CX, 2 * CY), BF16), pltpu.SemaphoreType.DMA((2,)), pltpu.SemaphoreType.DMA((2,)),
        ],
        compiler_params=params(collective_id=3, has_side_effects=True),
    )(values, pos1, pos2, state, slot)


def body(temp, cond, vx, vy, slot, lateral, dest, coef, prior):
    slot, lateral, dest, coef, prior = (v.reshape(FROWS, 128) for v in (slot, lateral, dest, coef, prior))
    t_fluid, total, ext, pos1, pos2, t3 = fluid(temp, cond, vx, vy, slot, coef, prior, lateral, dest)
    counts, lists = make_lists(t3)
    f3 = face_flux(total, slot, coef, prior, pos1, pos2, counts)
    source = wall_source(counts, lists, t3, f3)
    t_new = solid_steps(source, t_fluid, ext)
    values, t_new = wall_values(counts, lists, t3, t_new)
    wall = back(values, pos1, pos2, t_new, slot)
    return t_new, wall.reshape(FACES)


def solution(mesh):
    block, face = P("sec", "blk"), P(("sec", "blk"))
    in_specs = (block, block, block, block, face, P(("sec", "blk"), None), face, face, face)
    return jax.shard_map(body, mesh=mesh, in_specs=in_specs, out_specs=(block, face), check_vma=False)
```

time: 1460 us -> 170 us (0.12)
  the two profiles are of different devices: /device:TPU:15 before, /device:TPU:1 now
where the time goes in v2:
time: 170 us; the launch traced here: 169 us
  Pallas kernels  167 us (98%)
    pallas_call x1, Pallas kernels, back(): pl.pallas_call(back_kernel, out_shape=jax.ShapeDtypeStruct((FROWS, 128),...  67.1 us
    pallas_call x1, Pallas kernels, fluid(): pl.pallas_call(fluid_kernel, out_shape=[jax.ShapeDtypeStruct((CY, CX), F3...  63.4 us
    pallas_call x1, Pallas kernels, face_flux(): pl.pallas_call(flux_kernel, out_shape=jax.ShapeDtypeStruct((2 * ALLP + 8,...  28.2 us

profile of v2, /device:TPU:1, one launch (start us, length us, event | category | flops | bytes accessed | tf_op | source)
XLA Modules:
  0.0 169.3 jit_solution(1310403948386766426)
XLA Ops:
  0.6 63.4 %shard_map.104 = (f32[256,1024]{1,0:T(8,128)}, f32[8,256,128]{2,1,0:T(8,128)}, f32[7,9,304,128]{3,2,1,0:T(8,128)}, s32[64,128]{1,0:T(8,128)}, s32[128,128]{1,0:T(8,128)}, /*index=5*/s32[680,128]{1,0:T(8,128)}) custom-call(f32[256,1024]{1,0:T(8,128)} %temp.1, f32[256,1024]{1,0:T(8,128)} %cond.1, f32[256,1024]{1,0:T(8,128)} %vx.1, f32[256,1024]{1,0:T(8,128)} %vy.1, ...), custom_call_target="tpu_custom_call" | custom-call | tf_op jit(solution)/shard_map/pallas_call | solution.py:487
  64.0 1.6 shard_map.105
  65.6 28.2 %shard_map.106.f = f32[680,128]{1,0:T(8,128)} custom-call(f32[8,256,128]{2,1,0:T(8,128)} %get-tuple-element.15.total, s32[64,128]{1,0:T(8,128)} %bitcast.7, f32[64,128]{1,0:T(8,128)} %bitcast.10, f32[64,128]{1,0:T(8,128)} %bitcast.12, s32[64,128]{1,0:T(8,128)} %get-tuple-element.16.pos1, s32[128,128]{1,0:T(8,128)} %get-tuple-element.17.pos2, ...), custom_call_target="tpu_custom_call" | custom-call | tf_op jit(solution)/shard_map/pallas_call | solution.py:597
  93.8 1.9 %shard_map.107.source = f32[128,1024]{1,0:T(8,128)} custom-call(s32[8,128]{1,0:T(8,128)} %get-tuple-element.13.counts, s32[16,128]{1,0:T(8,128)} %get-tuple-element.14.lists, s32[680,128]{1,0:T(8,128)} %get-tuple-element.12.t, f32[680,128]{1,0:T(8,128)} %shard_map.106.f), custom_call_target="tpu_custom_call" | custom-call | tf_op jit(solution)/shard_map/pallas_call | solution.py:637
  95.8 2.5 %shard_map.108.state = f32[256,1024]{1,0:T(8,128)} custom-call(f32[128,1024]{1,0:T(8,128)} %shard_map.107.source, f32[256,1024]{1,0:T(8,128)} %get-tuple-element.18.t_fluid, f32[7,9,304,128]{3,2,1,0:T(8,128)} %get-tuple-element.19.ext), custom_call_target="tpu_custom_call" | custom-call | tf_op jit(solution)/shard_map/pallas_call | solution.py:751
  98.3 2.5 %shard_map.109 = (f32[680,128]{1,0:T(8,128)}, f32[256,1024]{1,0:T(8,128)}) custom-call(s32[8,128]{1,0:T(8,128)} %get-tuple-element.13.counts, s32[16,128]{1,0:T(8,128)} %get-tuple-element.14.lists, s32[680,128]{1,0:T(8,128)} %get-tuple-element.12.t, f32[256,1024]{1,0:T(8,128)} %shard_map.108.state), custom_call_target="tpu_custom_call" | custom-call | tf_op jit(solution)/shard_map/pallas_call | solution.py:674
  100.8 67.1 %shard_map.110 = f32[64,128]{1,0:T(8,128)} custom-call(f32[680,128]{1,0:T(8,128)} %get-tuple-element.21.values, s32[64,128]{1,0:T(8,128)} %get-tuple-element.16.pos1, s32[128,128]{1,0:T(8,128)} %get-tuple-element.17.pos2, f32[256,1024]{1,0:T(8,128)} %get-tuple-element.24.state, s32[64,128]{1,0:T(8,128)} %bitcast.8), custom_call_target="tpu_custom_call" | custom-call | tf_op jit(solution)/shard_map/pallas_call | solution.py:795
  168.0 1.4 copy.12

commit v3 on v2

--- a/solution.py
+++ b/solution.py
@@ -24,7 +24,7 @@
 PAIRS = 56
 CROWS = 2 * PAIRS
 ALLP = FLUID_ROWS * PAIRS
-QUAD = 4
+HEAT_PAIRS, WALL_PAIRS = 10, 8
 LROWS = 4
 HY, OY, TILES = 304, 24, 9
 VLIM = 60 << 20
@@ -237,12 +237,18 @@
         he, hw = h * (x[j] + east[j]), h * (x[j] + west[j])
         vx, vy = h * e[2, j, rows, :], h * e[3, j, rows, :]
         an, as_ = hn - vy, hs + vy
-        c0 = 1.0 - ((hn + hs) + (he + hw)) - DT * e[4, j, rows, :]
+        c0 = 1.0 - ((hn + hs) + (he + hw))
         c[0, j, rows, :] = jnp.where(last, 0.0, an)
         c[1, j, rows, :] = jnp.where(first, 0.0, as_)
         c[2, j, rows, :] = he - vx
         c[3, j, rows, :] = hw + vx
         c[4, j, rows, :] = c0 + jnp.where(first, as_, 0.0) + jnp.where(last, an, 0.0)
+
+
+def face_terms(e, c, r):
+    rows = pl.ds(r, 8)
+    for j in range(TILES):
+        c[4, j, rows, :] -= DT * e[4, j, rows, :]
         c[5, j, rows, :] = DT * e[5, j, rows, :]
 
 
@@ -386,11 +392,6 @@
 
         strips(strip, 1, 36, 4)
 
-    static_rows = rows_pair(0, 4, 0)
-    rows_start(static_rows)
-
-    acc[...] = jnp.zeros_like(acc)
-
     def maps(b, _):
         s, k = lane_row(slot, b, 8), lane_row(coef, b, 8)
         parts = split2(k) + split2(k * lane_row(prior, b, 8))
@@ -399,30 +400,34 @@
         acc[...] += dot_nt(a, onehot(iota((CX, 1024), 0) == (s & 1023)))
         return 0
 
-    lax.fori_loop(0, 4, maps, 0)
-    rows_wait(static_rows)
-    static_cols = cols_start(0, 4, 2, pack, land)
-    lax.fori_loop(4, 8, maps, 0)
-    for j in range(TILES - 1):
-        tile = slice(128 * j, 128 * j + 128)
-        e[4, j, mid, :] = acc[0:CY, tile] + acc[CY:2 * CY, tile]
-        e[5, j, mid, :] = acc[2 * CY:3 * CY, tile] + acc[3 * CY:4 * CY, tile]
-    map_rows = rows_pair(4, 2, 4)
-    rows_start(map_rows)
-    cols_wait(static_cols, 0, 4, land)
-
-    totals = ranks(lambda b: lane_row(lateral, b, 4), FROWS // 4, COLS, o_ref, p_ref)
-    carry = jnp.zeros((COLS, 128), F32)
-    for b in range(FROWS // 4):
-        put_lane_row(pos1, b, 4, lane_row(lateral, b, 4) * (BROWS * 128) + ranked(b, COLS, carry, o_ref, p_ref))
-        carry = carry + totals[b * COLS:(b + 1) * COLS]
-
-    rows_wait(map_rows)
-    map_cols = cols_start(4, 2, 6, packm, landm)
-    spread_all(pos1, lambda b: target_parts(lane_row(dest, b, 16) + 1024), 3, SLOTS, FROWS, tb_out)
+    static_rows, map_rows = rows_pair(0, 4, 0), rows_pair(4, 2, 4)
+
+    def place_maps():
+        for j in range(TILES - 1):
+            tile = slice(128 * j, 128 * j + 128)
+            e[4, j, mid, :] = acc[0:CY, tile] + acc[CY:2 * CY, tile]
+            e[5, j, mid, :] = acc[2 * CY:3 * CY, tile] + acc[3 * CY:4 * CY, tile]
+
+    def all_coefficients():
+        rows_start(map_rows)
+        strips(lambda r: coefficients(e, c, low, high, r), 1, 18, 3)
+        rows_wait(map_rows)
+        map_cols = cols_start(4, 2, 6, packm, landm)
+        strips(lambda r: coefficients(e, c, low, high, r), 19, 18, 3)
+        cols_wait(map_cols, 4, 2, landm)
+        strips(lambda r: face_terms(e, c, r), 1, 36, 4)
+
+    rows_start(static_rows)
+    acc[...] = jnp.zeros_like(acc)
 
     @pl.when(fluid)
     def _():
+        totals = ranks(lambda b: lane_row(lateral, b, 4), FROWS // 4, COLS, o_ref, p_ref)
+        carry = jnp.zeros((COLS, 128), F32)
+        for b in range(FROWS // 4):
+            put_lane_row(pos1, b, 4, lane_row(lateral, b, 4) * (BROWS * 128) + ranked(b, COLS, carry, o_ref, p_ref))
+            carry = carry + totals[b * COLS:(b + 1) * COLS]
+        spread_all(pos1, lambda b: target_parts(lane_row(dest, b, 16) + 1024), 3, SLOTS, FROWS, tb_out)
         tb[...] = target_join(tb_out[...], SLOTS)
 
         def one(q, _):
@@ -433,8 +438,32 @@
 
         lax.fori_loop(0, COLS, one, 0)
 
-    cols_wait(map_cols, 4, 2, landm)
-    strips(lambda r: coefficients(e, c, low, high, r), 1, 36, 4)
+    @pl.when(solid)
+    def _():
+        pos1[...] = jnp.zeros_like(pos1)
+
+    lax.fori_loop(0, 4, maps, 0)
+    rows_wait(static_rows)
+    static_cols = cols_start(0, 4, 2, pack, land)
+
+    @pl.when(fluid)
+    def _():
+        lax.fori_loop(4, 8, maps, 0)
+        place_maps()
+
+    @pl.when(solid)
+    def _():
+        arrive(tb_land, face_recv.at[0])
+        for i in range(3):
+            t = tb_land.at[pl.ds(i * SLOTS, SLOTS)]
+            compact(t, p2.at[i], t2.at[0, pl.ds(i * CROWS, CROWS)], o_ref, p_ref, t2_out)
+            push(p2.at[i], p2_land, face_send.at[1], face_recv.at[1], (mine + i, blk))
+        push(t2.at[0], t2.at[1], face_send.at[2], face_recv.at[2], (other, blk))
+        lax.fori_loop(4, 8, maps, 0)
+        place_maps()
+
+    cols_wait(static_cols, 0, 4, land)
+    all_coefficients()
 
     @pl.when(fluid)
     def _():
@@ -443,28 +472,24 @@
         for j in range(TILES - 1):
             t_out[:, 128 * j:128 * j + 128] = e[0, j, mid, :]
             s_out[j] = total[j, mid, :]
+        t3[...] = jnp.zeros_like(t3)
         arrive(tb, face_send.at[0])
         arrive(p2_land, face_recv.at[1])
         pos2[...] = p2_land[...]
-        t3[...] = jnp.zeros_like(t3)
 
     @pl.when(solid)
     def _():
-        first = pltpu.make_async_copy(e.at[0], ext.at[0], local.at[0])
         rest = pltpu.make_async_copy(c, ext.at[pl.ds(1, 6)], local.at[1])
+        rest.start()
+        strips(lambda r: advance(e.at[0], t_b, c, None, r), 1, 36, 6)
+        first = pltpu.make_async_copy(t_b, ext.at[0], local.at[0])
         first.start()
-        rest.start()
         t_out[...] = jnp.zeros_like(t_out)
         s_out[...] = jnp.zeros_like(s_out)
         pos2[...] = jnp.zeros_like(pos2)
-        arrive(tb_land, face_recv.at[0])
-        for i in range(3):
-            t = tb_land.at[pl.ds(i * SLOTS, SLOTS)]
-            compact(t, p2.at[i], t2.at[0, pl.ds(i * CROWS, CROWS)], o_ref, p_ref, t2_out)
-            push(p2.at[i], p2_land, face_send.at[1], face_recv.at[1], (mine + i, blk))
-        swap = push(t2.at[0], t2.at[1], face_send.at[2], face_recv.at[2], (other, blk))
         arrive(p2, face_send.at[1])
-        swap.wait()
+        arrive(t2.at[0], face_send.at[2])
+        arrive(t2.at[1], face_recv.at[2])
         half = 3 * CROWS
 
         @pl.when(sec == FLUID_ROWS)
@@ -547,10 +572,10 @@
     return lists[g * LROWS + (n >> 7), n & 127]
 
 
-def pair_row(ref, lists, g, i):
+def pair_row(ref, lists, g, i, n):
     rows = []
-    for j in range(QUAD):
-        p = listed(lists, g, QUAD * i + j)
+    for j in range(n):
+        p = listed(lists, g, n * i + j)
         rows += [ref[pl.ds(2 * p, 1), :], ref[pl.ds(2 * p + 1, 1), :]]
     return jnp.concatenate(rows, axis=1)
 
@@ -613,20 +638,21 @@
     @pl.when(sec >= FLUID_ROWS)
     def _():
         base = 128 * (sec - FLUID_ROWS) + 1
-        n = QUAD * 256
+        n = HEAT_PAIRS * 256
         for g in range(4):
             acc[...] = jnp.zeros_like(acc)
 
             def one(i, _):
-                v = pair_row(t, lists, g, i)
-                hi, lo = split2(pair_row(f, lists, g, i))
+                v = pair_row(t, lists, g, i, HEAT_PAIRS)
+                hi, lo = split2(pair_row(f, lists, g, i, HEAT_PAIRS))
                 hit = iota((128, n), 0) == (v >> 10) - base
                 a = jnp.concatenate([jnp.where(hit, p, 0.0).astype(BF16) for p in (hi, lo)], axis=0)
                 acc[...] += dot_nt(a, onehot(iota((256, n), 0) == (v & 255)))
                 return 0
 
-            lax.fori_loop(0, (counts[g, 0] + QUAD - 1) // QUAD, one, 0)
-            out[:, 256 * g:256 * (g + 1)] = acc[0:128] + acc[128:256]
+            lax.fori_loop(0, (counts[g, 0] + HEAT_PAIRS - 1) // HEAT_PAIRS, one, 0)
+            for h in range(2):
+                out[2 * g + h] = DT * (acc[0:128, 128 * h:128 * h + 128] + acc[128:256, 128 * h:128 * h + 128])
 
     @pl.when(sec < FLUID_ROWS)
     def _():
@@ -637,7 +663,7 @@
     return pl.pallas_call(
         source_kernel,
         in_specs=[pl.BlockSpec(memory_space=pltpu.SMEM)] * 2 + [pl.BlockSpec(memory_space=pltpu.VMEM)] * 2,
-        out_shape=jax.ShapeDtypeStruct((128, CX), F32),
+        out_shape=jax.ShapeDtypeStruct((TILES - 1, 128, 128), F32),
         scratch_shapes=[pltpu.VMEM((256, 256), F32)],
         compiler_params=params(),
     )(counts, lists, t, f)
@@ -651,23 +677,23 @@
     @pl.when(sec >= FLUID_ROWS)
     def _():
         base = 128 * (sec - FLUID_ROWS) + 1
-        n = QUAD * 256
+        n = WALL_PAIRS * 256
         for g in range(4):
             table = transposed_parts(state[0:128, 256 * g:256 * (g + 1)])
 
             def one(i, _):
-                v = pair_row(t, lists, g, i)
+                v = pair_row(t, lists, g, i, WALL_PAIRS)
                 r = onehot(iota((128, n), 0) == (v >> 10) - base)
                 x = dot(table, jnp.concatenate([r, r], axis=0))
                 x = jnp.where(((v >> 7) & 1) == 1, x[128:256], x[0:128])
                 x = jnp.sum(jnp.where(iota((128, n), 0) == (v & 127), x, 0.0), axis=0, keepdims=True)
-                for j in range(QUAD):
-                    p = listed(lists, g, QUAD * i + j)
+                for j in range(WALL_PAIRS):
+                    p = listed(lists, g, WALL_PAIRS * i + j)
                     out[pl.ds(2 * p, 1), :] = x[:, 256 * j:256 * j + 128]
                     out[pl.ds(2 * p + 1, 1), :] = x[:, 256 * j + 128:256 * j + 256]
                 return 0
 
-            lax.fori_loop(0, (counts[g, 0] + QUAD - 1) // QUAD, one, 0)
+            lax.fori_loop(0, (counts[g, 0] + WALL_PAIRS - 1) // WALL_PAIRS, one, 0)
 
 
 def wall_values(counts, lists, t, state):
@@ -679,7 +705,7 @@
     )(counts, lists, t, state)
 
 
-def solid_kernel(source, t_fluid, ext, t_out, e, c, x, pack, land, send, recv, local):
+def solid_kernel(heat, t_fluid, ext, t_out, e, c, side, below, corner, send, recv, local):
     sec, blk = lax.axis_index("sec"), lax.axis_index("blk")
     mid = slice(OY, OY + CY)
 
@@ -689,64 +715,72 @@
 
     @pl.when(sec >= FLUID_ROWS)
     def _():
+        upper, lower = FLUID_ROWS, SECS - 1
         left, right = lax.rem(blk + COLS - 1, COLS), lax.rem(blk + 1, COLS)
-        other = 2 * FLUID_ROWS + 1 - sec
-        for to in ((sec, left), (sec, right), (other, blk)):
-            signal(to)
         first = pltpu.make_async_copy(ext.at[0], e.at[0], local.at[0])
         rest = pltpu.make_async_copy(ext.at[pl.ds(1, 6)], c, local.at[1])
         first.start()
         rest.start()
-        for j in range(TILES):
-            x[j, 0:OY] = jnp.zeros((OY, 128), F32)
-            x[j, OY + 128:OY + CY] = jnp.zeros((CY - 128, 128), F32)
-        for j in range(TILES - 1):
-            x[j, OY:OY + 128] = DT * source[:, 128 * j:128 * j + 128]
-
-        @pl.when(sec == SECS - 1)
-        def _():
-            for j in range(TILES):
-                x[j, OY + CY:] = jnp.zeros((HY - OY - CY, 128), F32)
-
-        pl.semaphore_wait(pltpu.get_barrier_semaphore(), 3)
-        up = pltpu.make_async_remote_copy(
-            x.at[pl.ds(0, TILES - 1), pl.ds(OY, HALO)], x.at[pl.ds(0, TILES - 1), pl.ds(OY + CY, HALO)],
-            send.at[2], recv.at[2], device_id=(other, blk), device_id_type=MESH)
-
-        @pl.when(sec == SECS - 1)
-        def _():
-            up.start()
-            up.wait_send()
-
-        @pl.when(sec == FLUID_ROWS)
-        def _():
-            up.wait_recv()
-
-        parts = ((0, OY, 128), (128, OY + CY, HALO))
-        for at, fro, size in parts:
-            pack[0, at:at + size] = x[0, fro:fro + size]
-            pack[1, at:at + size] = x[TILES - 2, fro:fro + size]
-        to_left = push(pack.at[0], land.at[0], send.at[0], recv.at[0], (sec, left))
-        to_right = push(pack.at[1], land.at[1], send.at[1], recv.at[1], (sec, right))
-        to_left.wait()
-        to_right.wait()
-        for at, fro, size in parts:
-            x[TILES - 1, fro:fro + size] = jnp.where(iota((size, 128), 1) < 64, land[0, at:at + size], land[1, at:at + size])
+        signal((sec, left))
+        signal((sec, right))
+
+        @pl.when(sec == upper)
+        def _():
+            for q in (left, blk, right):
+                signal((lower, q))
+
+        pl.semaphore_wait(pltpu.get_barrier_semaphore(), jnp.where(sec == upper, 2, 5))
+        end = TILES - 2
+        copies = [push(heat.at[0], side.at[0], send.at[0], recv.at[0], (sec, left)),
+                  push(heat.at[end], side.at[1], send.at[1], recv.at[1], (sec, right))]
+        top = pl.ds(0, HALO)
+        down = [
+            pltpu.make_async_remote_copy(heat.at[pl.ds(0, TILES - 1), top], below, send.at[2], recv.at[2],
+                                         device_id=(upper, blk), device_id_type=MESH),
+            pltpu.make_async_remote_copy(heat.at[0, top], corner.at[0], send.at[3], recv.at[3],
+                                         device_id=(upper, left), device_id_type=MESH),
+            pltpu.make_async_remote_copy(heat.at[end, top], corner.at[1], send.at[4], recv.at[4],
+                                         device_id=(upper, right), device_id_type=MESH)]
+
+        @pl.when(sec == lower)
+        def _():
+            for d in down:
+                d.start()
+
         first.wait()
         rest.wait()
 
-        def drive(r):
-            rows = pl.ds(r, 8)
-            for j in range(TILES):
-                c[5, j, rows, :] += x[j, rows, :]
-
-        strips(drive, 2, 34, 2)
-        substeps(e.at[0], e.at[1], c, None, SOLID_STEPS)
+        def warm(j, rows, x):
+            e[0, j, rows, :] += x
+            c[5, j, rows, :] += x
+
         for j in range(TILES - 1):
-            t_out[:, 128 * j:128 * j + 128] = e[0, j, mid, :]
-
-
-def solid_steps(source, t_fluid, ext):
+            warm(j, slice(OY, OY + 128), heat[j])
+        for d in copies:
+            d.wait()
+        warm(TILES - 1, slice(OY, OY + 128), jnp.where(iota((128, 128), 1) < 64, side[0], side[1]))
+
+        @pl.when(sec == lower)
+        def _():
+            for d in down:
+                d.wait_send()
+
+        @pl.when(sec == upper)
+        def _():
+            for d in down:
+                d.wait_recv()
+            last = slice(OY + CY, OY + CY + HALO)
+            for j in range(TILES - 1):
+                warm(j, last, below[j])
+            warm(TILES - 1, last, jnp.where(iota((HALO, 128), 1) < 64, corner[0], corner[1]))
+
+        for n in range(SOLID_STEPS - 1):
+            strips(lambda r: advance(e.at[n % 2], e.at[1 - n % 2], c, None, r), 1, 36, 6)
+        for j in range(TILES - 1):
+            t_out[:, 128 * j:128 * j + 128] = e[(SOLID_STEPS - 1) % 2, j, mid, :]
+
+
+def solid_steps(heat, t_fluid, ext):
     vm = pl.BlockSpec(memory_space=pltpu.VMEM)
     return pl.pallas_call(
         solid_kernel,
@@ -754,12 +788,12 @@
         in_specs=[vm, vm, pl.BlockSpec(memory_space=pl.ANY)],
         out_specs=vm,
         scratch_shapes=[
-            pltpu.VMEM((2, TILES, HY, 128), F32), pltpu.VMEM((6, TILES, HY, 128), F32), pltpu.VMEM((TILES, HY, 128), F32),
-            pltpu.VMEM((2, 144, 128), F32), pltpu.VMEM((2, 144, 128), F32),
-            pltpu.SemaphoreType.DMA((3,)), pltpu.SemaphoreType.DMA((3,)), pltpu.SemaphoreType.DMA((2,)),
+            pltpu.VMEM((2, TILES, HY, 128), F32), pltpu.VMEM((6, TILES, HY, 128), F32),
+            pltpu.VMEM((2, 128, 128), F32), pltpu.VMEM((TILES - 1, HALO, 128), F32), pltpu.VMEM((2, HALO, 128), F32),
+            pltpu.SemaphoreType.DMA((5,)), pltpu.SemaphoreType.DMA((5,)), pltpu.SemaphoreType.DMA((2,)),
         ],
         compiler_params=params(collective_id=2, has_side_effects=True),
-    )(source, t_fluid, ext)
+    )(heat, t_fluid, ext)
 
 
 def back_kernel(values, pos1, pos2, state, slot, out, reply, fb, land, st, send, recv):

time: 170 us -> 156 us (0.918)
  Pallas kernels: 167 us -> 153 us
    pallas_call x1, Pallas kernels: 67.1 us -> 52.8 us  [back(): pl.pallas_call(back_kernel, out_shape=jax.ShapeDtypeStruct((FROWS, 128),...]
    pallas_call x1, Pallas kernels: 63.4 us -> 67 us  [fluid(): pl.pallas_call(fluid_kernel, out_shape=[jax.ShapeDtypeStruct((CY, CX), F3...]
    pallas_call x1, Pallas kernels: 28.2 us -> 24.8 us  [face_flux(): pl.pallas_call(flux_kernel, out_shape=jax.ShapeDtypeStruct((2 * ALLP + 8,...]
where the time goes in v3:
time: 156 us; the launch traced here: 155 us
  Pallas kernels  153 us (98%)
    pallas_call x1, Pallas kernels, fluid(): pl.pallas_call(fluid_kernel, out_shape=[jax.ShapeDtypeStruct((CY, CX), F3...  67 us
    pallas_call x1, Pallas kernels, back(): pl.pallas_call(back_kernel, out_shape=jax.ShapeDtypeStruct((FROWS, 128),...  52.8 us
    pallas_call x1, Pallas kernels, face_flux(): pl.pallas_call(flux_kernel, out_shape=jax.ShapeDtypeStruct((2 * ALLP + 8,...  24.8 us

profile of v3, /device:TPU:1, one launch (start us, length us, event | category | flops | bytes accessed | tf_op | source)
XLA Modules:
  0.0 155.3 jit_solution(2932110091797164888)
XLA Ops:
  0.6 67.0 %shard_map.104 = (f32[256,1024]{1,0:T(8,128)}, f32[8,256,128]{2,1,0:T(8,128)}, f32[7,9,304,128]{3,2,1,0:T(8,128)}, s32[64,128]{1,0:T(8,128)}, s32[128,128]{1,0:T(8,128)}, /*index=5*/s32[680,128]{1,0:T(8,128)}) custom-call(f32[256,1024]{1,0:T(8,128)} %temp.1, f32[256,1024]{1,0:T(8,128)} %cond.1, f32[256,1024]{1,0:T(8,128)} %vx.1, f32[256,1024]{1,0:T(8,128)} %vy.1, ...), custom_call_target="tpu_custom_call" | custom-call | tf_op jit(solution)/shard_map/pallas_call | solution.py:512
  67.6 1.6 %shard_map.105 = (s32[8,128]{1,0:T(8,128)}, s32[16,128]{1,0:T(8,128)}) custom-call(s32[680,128]{1,0:T(8,128)} %get-tuple-element.12.t), custom_call_target="tpu_custom_call" | custom-call | tf_op jit(solution)/shard_map/pallas_call | solution.py:564
  69.2 24.8 %shard_map.106.f = f32[680,128]{1,0:T(8,128)} custom-call(f32[8,256,128]{2,1,0:T(8,128)} %get-tuple-element.15.total, s32[64,128]{1,0:T(8,128)} %bitcast.7, f32[64,128]{1,0:T(8,128)} %bitcast.10, f32[64,128]{1,0:T(8,128)} %bitcast.12, s32[64,128]{1,0:T(8,128)} %get-tuple-element.16.pos1, s32[128,128]{1,0:T(8,128)} %get-tuple-element.17.pos2, ...), custom_call_target="tpu_custom_call" | custom-call | tf_op jit(solution)/shard_map/pallas_call | solution.py:622
  94.0 1.9 %shard_map.107.heat = f32[8,128,128]{2,1,0:T(8,128)} custom-call(s32[8,128]{1,0:T(8,128)} %get-tuple-element.13.counts, s32[16,128]{1,0:T(8,128)} %get-tuple-element.14.lists, s32[680,128]{1,0:T(8,128)} %get-tuple-element.12.t, f32[680,128]{1,0:T(8,128)} %shard_map.106.f), custom_call_target="tpu_custom_call" | custom-call | tf_op jit(solution)/shard_map/pallas_call | solution.py:663
  95.9 2.6 %shard_map.108.state = f32[256,1024]{1,0:T(8,128)} custom-call(f32[8,128,128]{2,1,0:T(8,128)} %shard_map.107.heat, f32[256,1024]{1,0:T(8,128)} %get-tuple-element.18.t_fluid, f32[7,9,304,128]{3,2,1,0:T(8,128)} %get-tuple-element.19.ext), custom_call_target="tpu_custom_call" | custom-call | tf_op jit(solution)/shard_map/pallas_call | solution.py:785
  98.5 2.5 %shard_map.109 = (f32[680,128]{1,0:T(8,128)}, f32[256,1024]{1,0:T(8,128)}) custom-call(s32[8,128]{1,0:T(8,128)} %get-tuple-element.13.counts, s32[16,128]{1,0:T(8,128)} %get-tuple-element.14.lists, s32[680,128]{1,0:T(8,128)} %get-tuple-element.12.t, f32[256,1024]{1,0:T(8,128)} %shard_map.108.state), custom_call_target="tpu_custom_call" | custom-call | tf_op jit(solution)/shard_map/pallas_call | solution.py:700
  101.0 52.8 %shard_map.110 = f32[64,128]{1,0:T(8,128)} custom-call(f32[680,128]{1,0:T(8,128)} %get-tuple-element.21.values, s32[64,128]{1,0:T(8,128)} %get-tuple-element.16.pos1, s32[128,128]{1,0:T(8,128)} %get-tuple-element.17.pos2, f32[256,1024]{1,0:T(8,128)} %get-tuple-element.24.state, s32[64,128]{1,0:T(8,128)} %bitcast.8), custom_call_target="tpu_custom_call" | custom-call | tf_op jit(solution)/shard_map/pallas_call | solution.py:829
  153.9 1.4 copy.12

commit v4 on v3

--- a/solution.py
+++ b/solution.py
@@ -218,8 +218,8 @@
 
 def substeps(a, b, c, total, count):
     def two(i, _):
-        strips(lambda r: advance(a, b, c, total, r), 1, 36, 6)
-        strips(lambda r: advance(b, a, c, total, r), 1, 36, 6)
+        strips(lambda r: advance(a, b, c, total, r), 1, 36, 12)
+        strips(lambda r: advance(b, a, c, total, r), 1, 36, 12)
         return 0
 
     lax.fori_loop(0, count // 2, two, 0)
@@ -272,8 +272,24 @@
     t2[...] = target_join(out[...], CROWS)
 
 
+def list_pairs(t, counts, lists, mine):
+    n = 768
+    v = jnp.concatenate([t[...].T[0:8], jnp.zeros((8, n - 2 * ALLP - 8), I32)], axis=1)[0:1]
+    row = iota((1, n), 1)
+    ours = (v >= 1024) & (((v - 1024) >> 17) == mine) & ((row & 1) == 0)
+    group = jnp.where(ours, (v >> 8) & 3, -1)
+    member = jnp.where(iota((8, n), 0) == group, 1.0, 0.0)
+    before = dot(member.astype(BF16), onehot(iota((n, n), 0) < iota((n, n), 1)))
+    rank = jnp.sum(member * before, axis=0, keepdims=True).astype(I32)
+    pos = jnp.where(ours, group * (LROWS * 128) + rank, -1)
+    back = (row >> 1) - ALLP
+    x = spread_rows(pos, ((back >> 1).astype(F32), (back & 1).astype(F32)), 4 * LROWS)
+    lists[...] = (2.0 * x[0:4 * LROWS] + x[4 * LROWS:]).astype(I32) + ALLP
+    counts[...] = dot(member.astype(BF16), onehot(iota((n, 128), 0) >= 0)).astype(I32)
+
+
 def fluid_kernel(temp, cond, vx, vy, slot, coef, prior, lateral, dest,
-                 t_out, s_out, ext, pos1, pos2, t3,
+                 t_out, s_out, ext, pos1, pos2, t3, counts, lists,
                  e, t_b, c, total, acc, pack, land, packm, landm, tb, tb_land, p2, p2_land, t2, o_ref, p_ref, tb_out, t2_out,
                  send, recv, face_send, face_recv, local):
     sec, blk = lax.axis_index("sec"), lax.axis_index("blk")
@@ -292,11 +308,13 @@
 
     @pl.when(has_low)
     def _():
-        signal((sec - 1, blk))
+        for q in (left, blk, right):
+            signal((sec - 1, q))
 
     @pl.when(has_high)
     def _():
-        signal((sec + 1, blk))
+        for q in (left, blk, right):
+            signal((sec + 1, q))
 
     @pl.when(fluid)
     def _():
@@ -324,43 +342,45 @@
         for a in range(6):
             for j in range(TILES - 1):
                 e[a, j, OY - HALO:OY, :] = jnp.zeros((HALO, 128), F32)
+        for ref in (land, landm):
+            ref[:, OY - HALO:OY, :] = jnp.zeros((2, HALO, 128), F32)
 
     @pl.when(high)
     def _():
         for a in range(6):
             for j in range(TILES - 1):
                 e[a, j, OY + CY:OY + CY + HALO, :] = jnp.zeros((HALO, 128), F32)
+        for ref in (land, landm):
+            ref[:, OY + CY:OY + CY + HALO, :] = jnp.zeros((2, HALO, 128), F32)
 
     pl.semaphore_wait(
         pltpu.get_barrier_semaphore(),
-        4 - low.astype(I32) - high.astype(I32) + jnp.where(fluid, COLS, 3))
-
-    def rows_copy(first, arrays, src, dst, i, to):
-        return pltpu.make_async_remote_copy(
-            e.at[pl.ds(first, arrays), pl.ds(0, TILES - 1), pl.ds(src, HALO)],
-            e.at[pl.ds(first, arrays), pl.ds(0, TILES - 1), pl.ds(dst, HALO)],
-            send.at[i], recv.at[i], device_id=to, device_id_type=MESH)
-
-    def rows_pair(first, arrays, i):
-        return (rows_copy(first, arrays, OY, OY + CY, i, (sec - 1, blk)),
-                rows_copy(first, arrays, OY + CY - HALO, OY - HALO, i + 1, (sec + 1, blk)))
-
-    def rows_start(pair):
-        pl.when(has_low)(pair[0].start)
-        pl.when(has_high)(pair[1].start)
-
-    def rows_wait(pair):
-        @pl.when(has_low)
-        def _():
-            pair[0].wait_send()
-            pair[1].wait_recv()
-
-        @pl.when(has_high)
-        def _():
-            pair[1].wait_send()
-            pair[0].wait_recv()
-
-    def cols_start(first, arrays, i, pack, land):
+        8 - 3 * (low.astype(I32) + high.astype(I32)) + jnp.where(fluid, COLS, 3))
+
+    first_rows, last_rows = pl.ds(OY, HALO), pl.ds(OY + CY - HALO, HALO)
+    below, above = pl.ds(OY + CY, HALO), pl.ds(OY - HALO, HALO)
+
+    def halo_copies(first, arrays, i, pack, land):
+        count = [0]
+
+        def copy(src, dst, to):
+            at = i + count[0]
+            count[0] += 1
+            return pltpu.make_async_remote_copy(src, dst, send.at[at], recv.at[at], device_id=to, device_id_type=MESH)
+
+        body = e.at[pl.ds(first, arrays), pl.ds(0, TILES - 1)]
+        up = [copy(body.at[:, :, first_rows], body.at[:, :, below], (sec - 1, blk))]
+        down = [copy(body.at[:, :, last_rows], body.at[:, :, above], (sec + 1, blk))]
+        here = []
+        for side, to in ((0, left), (1, right)):
+            own, there = pack.at[side], land.at[side]
+            here.append(copy(own.at[pl.ds(OY, CY)], there.at[pl.ds(OY, CY)], (sec, to)))
+            up.append(copy(own.at[first_rows], there.at[below], (sec - 1, to)))
+            down.append(copy(own.at[last_rows], there.at[above], (sec + 1, to)))
+        return here, up, down
+
+    def halo_start(copies, first, arrays, pack):
+        here, up, down = copies
         lane = iota((8, 128), 1)
 
         def strip(r):
@@ -368,19 +388,47 @@
             lo = e[first, 0, rows, :]
             hi = lane_roll(e[first, TILES - 2, rows, :], HALO)
             for a in range(1, arrays):
-                here = (lane >> 4) == a
-                lo = jnp.where(here, lane_roll(e[first + a, 0, rows, :], HALO * a), lo)
-                hi = jnp.where(here, lane_roll(e[first + a, TILES - 2, rows, :], HALO * a + HALO), hi)
+                mine = (lane >> 4) == a
+                lo = jnp.where(mine, lane_roll(e[first + a, 0, rows, :], HALO * a), lo)
+                hi = jnp.where(mine, lane_roll(e[first + a, TILES - 2, rows, :], HALO * a + HALO), hi)
             pack[0, rows, :] = lo
             pack[1, rows, :] = hi
 
-        strips(strip, 1, 36, 4)
-        return (push(pack.at[0, pl.ds(8, 288)], land.at[0, pl.ds(8, 288)], send.at[i], recv.at[i], (sec, left)),
-                push(pack.at[1, pl.ds(8, 288)], land.at[1, pl.ds(8, 288)], send.at[i + 1], recv.at[i + 1], (sec, right)))
-
-    def cols_wait(pair, first, arrays, land):
-        pair[0].wait()
-        pair[1].wait()
+        pl.when(has_low)(up[0].start)
+        pl.when(has_high)(down[0].start)
+        strips(strip, 3, 32, 8)
+        for d in here:
+            d.start()
+
+        @pl.when(has_low)
+        def _():
+            for d in up[1:]:
+                d.start()
+
+        @pl.when(has_high)
+        def _():
+            for d in down[1:]:
+                d.start()
+
+    def halo_wait(copies, first, arrays, land):
+        here, up, down = copies
+        for d in here:
+            d.wait()
+
+        @pl.when(has_low)
+        def _():
+            for d in up:
+                d.wait_send()
+            for d in down:
+                d.wait_recv()
+
+        @pl.when(has_high)
+        def _():
+            for d in down:
+                d.wait_send()
+            for d in up:
+                d.wait_recv()
+
         lane = iota((8, 128), 1)
 
         def strip(r):
@@ -390,7 +438,7 @@
                 e[first + a, TILES - 1, rows, :] = jnp.where(
                     lane < 64, lane_roll(lo, -HALO * a), lane_roll(hi, 128 - HALO - HALO * a))
 
-        strips(strip, 1, 36, 4)
+        strips(strip, 1, 36, 6)
 
     def maps(b, _):
         s, k = lane_row(slot, b, 8), lane_row(coef, b, 8)
@@ -400,7 +448,7 @@
         acc[...] += dot_nt(a, onehot(iota((CX, 1024), 0) == (s & 1023)))
         return 0
 
-    static_rows, map_rows = rows_pair(0, 4, 0), rows_pair(4, 2, 4)
+    static, of_maps = halo_copies(0, 4, 0, pack, land), halo_copies(4, 2, 8, packm, landm)
 
     def place_maps():
         for j in range(TILES - 1):
@@ -408,16 +456,7 @@
             e[4, j, mid, :] = acc[0:CY, tile] + acc[CY:2 * CY, tile]
             e[5, j, mid, :] = acc[2 * CY:3 * CY, tile] + acc[3 * CY:4 * CY, tile]
 
-    def all_coefficients():
-        rows_start(map_rows)
-        strips(lambda r: coefficients(e, c, low, high, r), 1, 18, 3)
-        rows_wait(map_rows)
-        map_cols = cols_start(4, 2, 6, packm, landm)
-        strips(lambda r: coefficients(e, c, low, high, r), 19, 18, 3)
-        cols_wait(map_cols, 4, 2, landm)
-        strips(lambda r: face_terms(e, c, r), 1, 36, 4)
-
-    rows_start(static_rows)
+    halo_start(static, 0, 4, pack)
     acc[...] = jnp.zeros_like(acc)
 
     @pl.when(fluid)
@@ -443,8 +482,6 @@
         pos1[...] = jnp.zeros_like(pos1)
 
     lax.fori_loop(0, 4, maps, 0)
-    rows_wait(static_rows)
-    static_cols = cols_start(0, 4, 2, pack, land)
 
     @pl.when(fluid)
     def _():
@@ -462,8 +499,11 @@
         lax.fori_loop(4, 8, maps, 0)
         place_maps()
 
-    cols_wait(static_cols, 0, 4, land)
-    all_coefficients()
+    halo_start(of_maps, 4, 2, packm)
+    halo_wait(static, 0, 4, land)
+    strips(lambda r: coefficients(e, c, low, high, r), 1, 36, 4)
+    halo_wait(of_maps, 4, 2, landm)
+    strips(lambda r: face_terms(e, c, r), 1, 36, 4)
 
     @pl.when(fluid)
     def _():
@@ -473,6 +513,8 @@
             t_out[:, 128 * j:128 * j + 128] = e[0, j, mid, :]
             s_out[j] = total[j, mid, :]
         t3[...] = jnp.zeros_like(t3)
+        counts[...] = jnp.zeros_like(counts)
+        lists[...] = jnp.zeros_like(lists)
         arrive(tb, face_send.at[0])
         arrive(p2_land, face_recv.at[1])
         pos2[...] = p2_land[...]
@@ -503,6 +545,7 @@
             t3[half:2 * half] = t2[0]
 
         t3[2 * half:] = jnp.zeros((8, 128), I32)
+        list_pairs(t3, counts, lists, sec - FLUID_ROWS)
         first.wait()
         rest.wait()
 
@@ -516,9 +559,10 @@
             jax.ShapeDtypeStruct((7, TILES, HY, 128), F32),
             jax.ShapeDtypeStruct((FROWS, 128), I32), jax.ShapeDtypeStruct((SLOTS, 128), I32),
             jax.ShapeDtypeStruct((2 * ALLP + 8, 128), I32),
+            jax.ShapeDtypeStruct((8, 128), I32), jax.ShapeDtypeStruct((4 * LROWS, 128), I32),
         ],
         in_specs=[vm] * 9,
-        out_specs=[vm, vm, pl.BlockSpec(memory_space=pl.ANY), vm, vm, vm],
+        out_specs=[vm, vm, pl.BlockSpec(memory_space=pl.ANY)] + [vm] * 5,
         scratch_shapes=[
             pltpu.VMEM((6, TILES, HY, 128), F32), pltpu.VMEM((TILES, HY, 128), F32), pltpu.VMEM((6, TILES, HY, 128), F32),
             pltpu.VMEM((TILES - 1, HY, 128), F32), pltpu.VMEM((4 * CY, CX), F32),
@@ -528,44 +572,11 @@
             pltpu.VMEM((3, SLOTS, 128), I32), pltpu.VMEM((SLOTS, 128), I32), pltpu.VMEM((2, 3 * CROWS, 128), I32),
             pltpu.VMEM((256, KR), F32), pltpu.VMEM((256, KR), F32),
             pltpu.VMEM((3 * SLOTS, 128), F32), pltpu.VMEM((3 * CROWS, 128), F32),
-            pltpu.SemaphoreType.DMA((8,)), pltpu.SemaphoreType.DMA((8,)),
+            pltpu.SemaphoreType.DMA((16,)), pltpu.SemaphoreType.DMA((16,)),
             pltpu.SemaphoreType.DMA((3,)), pltpu.SemaphoreType.DMA((3,)), pltpu.SemaphoreType.DMA((2,)),
         ],
         compiler_params=params(collective_id=0, has_side_effects=True),
     )(temp, cond, vx, vy, slot, coef, prior, lateral, dest)
-
-
-def list_kernel(t, counts, lists):
-    sec = lax.axis_index("sec")
-
-    @pl.when(sec < FLUID_ROWS)
-    def _():
-        counts[...] = jnp.zeros_like(counts)
-        lists[...] = jnp.zeros_like(lists)
-
-    @pl.when(sec >= FLUID_ROWS)
-    def _():
-        n = 768
-        v = jnp.concatenate([t[...].T[0:8], jnp.zeros((8, n - 2 * ALLP - 8), I32)], axis=1)[0:1]
-        row = iota((1, n), 1)
-        ours = (v >= 1024) & (((v - 1024) >> 17) == sec - FLUID_ROWS) & ((row & 1) == 0)
-        group = jnp.where(ours, (v >> 8) & 3, -1)
-        member = jnp.where(iota((8, n), 0) == group, 1.0, 0.0)
-        before = dot(member.astype(BF16), onehot(iota((n, n), 0) < iota((n, n), 1)))
-        rank = jnp.sum(member * before, axis=0, keepdims=True).astype(I32)
-        pos = jnp.where(ours, group * (LROWS * 128) + rank, -1)
-        back = (row >> 1) - ALLP
-        x = spread_rows(pos, ((back >> 1).astype(F32), (back & 1).astype(F32)), 4 * LROWS)
-        lists[...] = (2.0 * x[0:4 * LROWS] + x[4 * LROWS:]).astype(I32) + ALLP
-        counts[...] = dot(member.astype(BF16), onehot(iota((n, 128), 0) >= 0)).astype(I32)
-
-
-def make_lists(t):
-    return pl.pallas_call(
-        list_kernel,
-        out_shape=[jax.ShapeDtypeStruct((8, 128), I32), jax.ShapeDtypeStruct((4 * LROWS, 128), I32)],
-        compiler_params=params(),
-    )(t)
 
 
 def listed(lists, g, n):
@@ -580,7 +591,7 @@
     return jnp.concatenate(rows, axis=1)
 
 
-def flux_kernel(total, slot, coef, prior, pos1, pos2, counts, f3, st, fb, land, f2, f3_land, spread, send, recv):
+def flux_kernel(total, slot, coef, prior, pos1, pos2, f3, st, fb, land, f2, f3_land, spread, send, recv):
     sec, blk = lax.axis_index("sec"), lax.axis_index("blk")
 
     @pl.when(sec < FLUID_ROWS)
@@ -618,18 +629,18 @@
         f3[2 * ALLP:] = jnp.zeros((8, 128), F32)
 
 
-def face_flux(total, slot, coef, prior, pos1, pos2, counts):
+def face_flux(total, slot, coef, prior, pos1, pos2):
     return pl.pallas_call(
         flux_kernel,
         out_shape=jax.ShapeDtypeStruct((2 * ALLP + 8, 128), F32),
-        in_specs=[pl.BlockSpec(memory_space=pltpu.VMEM)] * 6 + [pl.BlockSpec(memory_space=pl.ANY)],
+        in_specs=[pl.BlockSpec(memory_space=pltpu.VMEM)] * 6,
         scratch_shapes=[
             pltpu.VMEM((CX, 2 * CY), BF16), pltpu.VMEM((SLOTS, 128), F32), pltpu.VMEM((SLOTS, 128), F32),
             pltpu.VMEM((CROWS, 128), F32), pltpu.VMEM((2 * ALLP, 128), F32), pltpu.VMEM((2 * SLOTS, 128), F32),
             pltpu.SemaphoreType.DMA((3,)), pltpu.SemaphoreType.DMA((2,)),
         ],
         compiler_params=params(collective_id=1, has_side_effects=True),
-    )(total, slot, coef, prior, pos1, pos2, counts)
+    )(total, slot, coef, prior, pos1, pos2)
 
 
 def source_kernel(counts, lists, t, f, out, acc):
@@ -775,7 +786,7 @@
             warm(TILES - 1, last, jnp.where(iota((HALO, 128), 1) < 64, corner[0], corner[1]))
 
         for n in range(SOLID_STEPS - 1):
-            strips(lambda r: advance(e.at[n % 2], e.at[1 - n % 2], c, None, r), 1, 36, 6)
+            strips(lambda r: advance(e.at[n % 2], e.at[1 - n % 2], c, None, r), 1, 36, 12)
         for j in range(TILES - 1):
             t_out[:, 128 * j:128 * j + 128] = e[(SOLID_STEPS - 1) % 2, j, mid, :]
 
@@ -840,9 +851,8 @@
 
 def body(temp, cond, vx, vy, slot, lateral, dest, coef, prior):
     slot, lateral, dest, coef, prior = (v.reshape(FROWS, 128) for v in (slot, lateral, dest, coef, prior))
-    t_fluid, total, ext, pos1, pos2, t3 = fluid(temp, cond, vx, vy, slot, coef, prior, lateral, dest)
-    counts, lists = make_lists(t3)
-    f3 = face_flux(total, slot, coef, prior, pos1, pos2, counts)
+    t_fluid, total, ext, pos1, pos2, t3, counts, lists = fluid(temp, cond, vx, vy, slot, coef, prior, lateral, dest)
+    f3 = face_flux(total, slot, coef, prior, pos1, pos2)
     source = wall_source(counts, lists, t3, f3)
     t_new = solid_steps(source, t_fluid, ext)
     values, t_new = wall_values(counts, lists, t3, t_new)

time: 156 us -> 149 us (0.955)
  Pallas kernels: 153 us -> 147 us
    pallas_call x1, Pallas kernels: 52.8 us -> 47.9 us  [back(): pl.pallas_call(back_kernel, out_shape=jax.ShapeDtypeStruct((FROWS, 128),...]
    pallas_call x1, Pallas kernels: 24.8 us -> 29 us  [face_flux(): pl.pallas_call(flux_kernel, out_shape=jax.ShapeDtypeStruct((2 * ALLP + 8,...]
    pallas_call x1, Pallas kernels: 67 us -> 63.2 us  [fluid(): pl.pallas_call(fluid_kernel, out_shape=[jax.ShapeDtypeStruct((CY, CX), F3...]
    pallas_call x1 -> x0, Pallas kernels: 1.59 us -> none  [make_lists(): pl.pallas_call(list_kernel, out_shape=[jax.ShapeDtypeStruct((8, 128), I32...]
where the time goes in v4:
time: 149 us
  Pallas kernels  147 us (99%)
    pallas_call x1, Pallas kernels, fluid(): pl.pallas_call(fluid_kernel, out_shape=[jax.ShapeDtypeStruct((CY, CX), F3...  63.2 us
    pallas_call x1, Pallas kernels, back(): pl.pallas_call(back_kernel, out_shape=jax.ShapeDtypeStruct((FROWS, 128),...  47.9 us
    pallas_call x1, Pallas kernels, face_flux(): pl.pallas_call(flux_kernel, out_shape=jax.ShapeDtypeStruct((2 * ALLP + 8,...  29 us

profile of v4, /device:TPU:1, one launch (start us, length us, event | category | flops | bytes accessed | tf_op | source)
XLA Modules:
  0.0 149.1 jit_solution(2427978870080151734)
XLA Ops:
  0.6 63.2 %shard_map.104 = (f32[256,1024]{1,0:T(8,128)}, f32[8,256,128]{2,1,0:T(8,128)}, f32[7,9,304,128]{3,2,1,0:T(8,128)}, s32[64,128]{1,0:T(8,128)}, s32[128,128]{1,0:T...) custom-call(f32[256,1024]{1,0:T(8,128)} %temp.1, f32[256,1024]{1,0:T(8,128)} %cond.1, ...), custom_call_target="tpu_custom_call" | custom-call | tf_op jit(solution)/shard_map/pallas_call | solution.py:555
  63.8 29.0 %shard_map.105.f = f32[680,128]{1,0:T(8,128)} custom-call(f32[8,256,128]{2,1,0:T(8,128)} %get-tuple-element.15.total, s32[64,128]{1,0:T(8,128)} %bitcast.7, f32[64,128]{1,0:T(8,128)} %bitcast.10, f32[64,128]{1,0:T(8,128)} %bitcast.12, s32[64,128]{1,0:T(8,128)} %get-tuple-element.16.pos1, s32[128,128]{1,0:T(8,128)} %get-tuple-element.17.pos2), custom_call_target="tpu_custom_call" | custom-call | tf_op jit(solution)/shard_map/pallas_call | solution.py:633
  92.8 1.9 %shard_map.106.heat = f32[8,128,128]{2,1,0:T(8,128)} custom-call(s32[8,128]{1,0:T(8,128)} %get-tuple-element.12.counts, s32[16,128]{1,0:T(8,128)} %get-tuple-element.13.lists, s32[680,128]{1,0:T(8,128)} %get-tuple-element.14.t, f32[680,128]{1,0:T(8,128)} %shard_map.105.f), custom_call_target="tpu_custom_call" | custom-call | tf_op jit(solution)/shard_map/pallas_call | solution.py:674
  94.7 2.5 %shard_map.107.state = f32[256,1024]{1,0:T(8,128)} custom-call(f32[8,128,128]{2,1,0:T(8,128)} %shard_map.106.heat, f32[256,1024]{1,0:T(8,128)} %get-tuple-element.18.t_fluid, f32[7,9,304,128]{3,2,1,0:T(8,128)} %get-tuple-element.19.ext), custom_call_target="tpu_custom_call" | custom-call | tf_op jit(solution)/shard_map/pallas_call | solution.py:796
  97.3 2.5 %shard_map.108 = (f32[680,128]{1,0:T(8,128)}, f32[256,1024]{1,0:T(8,128)}) custom-call(s32[8,128]{1,0:T(8,128)} %get-tuple-element.12.counts, s32[16,128]{1,0:T(8,128)} %get-tuple-element.13.lists, s32[680,128]{1,0:T(8,128)} %get-tuple-element.14.t, f32[256,1024]{1,0:T(8,128)} %shard_map.107.state), custom_call_target="tpu_custom_call" | custom-call | tf_op jit(solution)/shard_map/pallas_call | solution.py:711
  99.8 47.9 %shard_map.109 = f32[64,128]{1,0:T(8,128)} custom-call(f32[680,128]{1,0:T(8,128)} %get-tuple-element.21.values, s32[64,128]{1,0:T(8,128)} %get-tuple-element.16.pos1, s32[128,128]{1,0:T(8,128)} %get-tuple-element.17.pos2, f32[256,1024]{1,0:T(8,128)} %get-tuple-element.24.state, s32[64,128]{1,0:T(8,128)} %bitcast.8), custom_call_target="tpu_custom_call" | custom-call | tf_op jit(solution)/shard_map/pallas_call | solution.py:840
  147.7 1.4 copy.12

commit v5 on v4

--- a/solution.py
+++ b/solution.py
@@ -19,7 +19,7 @@
 FROWS = FACES // 128
 KR = 512
 HALO = 16
-BROWS = 8
+BROWS = 6
 SLOTS = COLS * BROWS
 PAIRS = 56
 CROWS = 2 * PAIRS
@@ -159,12 +159,12 @@
     def one(q, _):
         @pl.when(q != blk)
         def _():
-            push(src.at[pl.ds(pl.multiple_of(q * BROWS, 8), BROWS)], land.at[pl.ds(pl.multiple_of(blk * BROWS, 8), BROWS)],
+            push(src.at[pl.ds(q * BROWS, BROWS)], land.at[pl.ds(blk * BROWS, BROWS)],
                  send, recv, (sec, q))
         return 0
 
     lax.fori_loop(0, COLS, one, 0)
-    own = pl.ds(pl.multiple_of(blk * BROWS, 8), BROWS)
+    own = pl.ds(blk * BROWS, BROWS)
     land[own, :] = src[own, :]
     arrive(src.at[pl.ds(0, SLOTS - BROWS)], send)
     arrive(land.at[pl.ds(0, SLOTS - BROWS)], recv)
@@ -470,8 +470,8 @@
         tb[...] = target_join(tb_out[...], SLOTS)
 
         def one(q, _):
-            push(tb.at[pl.ds(pl.multiple_of(q * BROWS, 8), BROWS)],
-                 tb_land.at[pl.ds(pl.multiple_of(lax.rem(sec, 3) * SLOTS + blk * BROWS, 8), BROWS)],
+            push(tb.at[pl.ds(q * BROWS, BROWS)],
+                 tb_land.at[pl.ds(lax.rem(sec, 3) * SLOTS + blk * BROWS, BROWS)],
                  face_send.at[0], face_recv.at[0], (server, q))
             return 0
 
@@ -598,12 +598,13 @@
     def _():
         greet_peers(sec, blk)
         gather_cells(lambda j: total[j], st)
-        spread[...] = jnp.zeros_like(spread)
+        placed = spread.at[pl.ds(0, 2 * SLOTS)]
+        placed[...] = jnp.zeros((2 * SLOTS, 128), F32)
 
         def one(b, _):
             value = cell_values(st, lane_row(slot, b, 8)) * (1.0 / FLUID_STEPS)
             flux = lane_row(coef, b, 8) * (value - lane_row(prior, b, 8))
-            spread[...] += spread_rows(lane_row(pos1, b, 8), split2(flux), SLOTS)
+            placed[...] += spread_rows(lane_row(pos1, b, 8), split2(flux), SLOTS)
             return 0
 
         lax.fori_loop(0, FROWS // 8, one, 0)
@@ -636,7 +637,7 @@
         in_specs=[pl.BlockSpec(memory_space=pltpu.VMEM)] * 6,
         scratch_shapes=[
             pltpu.VMEM((CX, 2 * CY), BF16), pltpu.VMEM((SLOTS, 128), F32), pltpu.VMEM((SLOTS, 128), F32),
-            pltpu.VMEM((CROWS, 128), F32), pltpu.VMEM((2 * ALLP, 128), F32), pltpu.VMEM((2 * SLOTS, 128), F32),
+            pltpu.VMEM((CROWS, 128), F32), pltpu.VMEM((2 * ALLP, 128), F32), pltpu.VMEM((2 * CROWS, 128), F32),
             pltpu.SemaphoreType.DMA((3,)), pltpu.SemaphoreType.DMA((2,)),
         ],
         compiler_params=params(collective_id=1, has_side_effects=True),
@@ -680,10 +681,11 @@
     )(counts, lists, t, f)
 
 
-def wall_kernel(counts, lists, t, state, out, t_out):
+def wall_kernel(counts, lists, t, state, out, t_out, sem):
     sec = lax.axis_index("sec")
     out[...] = jnp.zeros_like(out)
-    t_out[...] = state[...]
+    whole = pltpu.make_async_copy(state, t_out, sem.at[0])
+    whole.start()
 
     @pl.when(sec >= FLUID_ROWS)
     def _():
@@ -706,23 +708,29 @@
 
             lax.fori_loop(0, (counts[g, 0] + WALL_PAIRS - 1) // WALL_PAIRS, one, 0)
 
+    whole.wait()
+
 
 def wall_values(counts, lists, t, state):
+    sm, vm, hbm = (pl.BlockSpec(memory_space=m) for m in (pltpu.SMEM, pltpu.VMEM, pl.ANY))
     return pl.pallas_call(
         wall_kernel,
-        in_specs=[pl.BlockSpec(memory_space=pltpu.SMEM)] * 2 + [pl.BlockSpec(memory_space=pltpu.VMEM)] * 2,
+        in_specs=[sm, sm, vm, vm],
+        out_specs=[vm, hbm],
         out_shape=[jax.ShapeDtypeStruct((2 * ALLP + 8, 128), F32), jax.ShapeDtypeStruct((CY, CX), F32)],
+        scratch_shapes=[pltpu.SemaphoreType.DMA((1,))],
         compiler_params=params(),
     )(counts, lists, t, state)
 
 
-def solid_kernel(heat, t_fluid, ext, t_out, e, c, side, below, corner, send, recv, local):
+def solid_kernel(heat, t_fluid, ext, t_out, e, c, side, below, corner, send, recv, local, finish):
     sec, blk = lax.axis_index("sec"), lax.axis_index("blk")
-    mid = slice(OY, OY + CY)
 
     @pl.when(sec < FLUID_ROWS)
     def _():
-        t_out[...] = t_fluid[...]
+        pass_on = pltpu.make_async_copy(t_fluid, t_out, local.at[0])
+        pass_on.start()
+        pass_on.wait()
 
     @pl.when(sec >= FLUID_ROWS)
     def _():
@@ -787,21 +795,25 @@
 
         for n in range(SOLID_STEPS - 1):
             strips(lambda r: advance(e.at[n % 2], e.at[1 - n % 2], c, None, r), 1, 36, 12)
-        for j in range(TILES - 1):
-            t_out[:, 128 * j:128 * j + 128] = e[(SOLID_STEPS - 1) % 2, j, mid, :]
+        done = [pltpu.make_async_copy(e.at[(SOLID_STEPS - 1) % 2, j, pl.ds(OY, CY)], t_out.at[:, pl.ds(128 * j, 128)], finish.at[j])
+                for j in range(TILES - 1)]
+        for d in done:
+            d.start()
+        for d in done:
+            d.wait()
 
 
 def solid_steps(heat, t_fluid, ext):
-    vm = pl.BlockSpec(memory_space=pltpu.VMEM)
+    vm, hbm = pl.BlockSpec(memory_space=pltpu.VMEM), pl.BlockSpec(memory_space=pl.ANY)
     return pl.pallas_call(
         solid_kernel,
         out_shape=jax.ShapeDtypeStruct((CY, CX), F32),
-        in_specs=[vm, vm, pl.BlockSpec(memory_space=pl.ANY)],
-        out_specs=vm,
+        in_specs=[vm, vm, hbm],
+        out_specs=hbm,
         scratch_shapes=[
             pltpu.VMEM((2, TILES, HY, 128), F32), pltpu.VMEM((6, TILES, HY, 128), F32),
             pltpu.VMEM((2, 128, 128), F32), pltpu.VMEM((TILES - 1, HALO, 128), F32), pltpu.VMEM((2, HALO, 128), F32),
-            pltpu.SemaphoreType.DMA((5,)), pltpu.SemaphoreType.DMA((5,)), pltpu.SemaphoreType.DMA((2,)),
+            pltpu.SemaphoreType.DMA((5,)), pltpu.SemaphoreType.DMA((5,)), pltpu.SemaphoreType.DMA((2,)), pltpu.SemaphoreType.DMA((TILES - 1,)),
         ],
         compiler_params=params(collective_id=2, has_side_effects=True),
     )(heat, t_fluid, ext)

time: 149 us -> 145 us (0.973)
  Pallas kernels: 147 us -> 143 us
    pallas_call x1, Pallas kernels: 47.9 us -> 45.1 us  [back(): pl.pallas_call(back_kernel, out_shape=jax.ShapeDtypeStruct((FROWS, 128),...]
where the time goes in v5:
time: 145 us
  Pallas kernels  143 us (99%)
    pallas_call x1, Pallas kernels, fluid(): pl.pallas_call(fluid_kernel, out_shape=[jax.ShapeDtypeStruct((CY, CX), F3...  62.4 us
    pallas_call x1, Pallas kernels, back(): pl.pallas_call(back_kernel, out_shape=jax.ShapeDtypeStruct((FROWS, 128),...  45.1 us
    pallas_call x1, Pallas kernels, face_flux(): pl.pallas_call(flux_kernel, out_shape=jax.ShapeDtypeStruct((2 * ALLP + 8,...  28 us
    pallas_call x1, Pallas kernels, wall_values(): pl.pallas_call(wall_kernel, in_specs=[sm, sm, vm, vm], out_specs=[vm, hbm...  3.06 us

profile of v5, /device:TPU:1, one launch (start us, length us, event | category | flops | bytes accessed | tf_op | source)
XLA Modules:
  0.0 145.1 jit_solution(2763500731738589714)
XLA Ops:
  0.6 62.4 %shard_map.104 = (f32[256,1024]{1,0:T(8,128)}, f32[8,256,128]{2,1,0:T(8,128)}, f32[7,9,304,128]{3,2,1,0:T(8,128)}, s32[64,128]{1,0:T(8,128)}, s32[96,128]{1,0:T(...) custom-call(f32[256,1024]{1,0:T(8,128)} %temp.1, f32[256,1024]{1,0:T(8,128)} %cond.1, ...), custom_call_target="tpu_custom_call" | custom-call | tf_op jit(solution)/shard_map/pallas_call | solution.py:555
  63.1 28.0 %shard_map.105.f = f32[680,128]{1,0:T(8,128)} custom-call(f32[8,256,128]{2,1,0:T(8,128)} %get-tuple-element.15.total, s32[64,128]{1,0:T(8,128)} %bitcast.7, f32[64,128]{1,0:T(8,128)} %bitcast.10, f32[64,128]{1,0:T(8,128)} %bitcast.12, s32[64,128]{1,0:T(8,128)} %get-tuple-element.16.pos1, s32[96,128]{1,0:T(8,128)} %get-tuple-element.17.pos2), custom_call_target="tpu_custom_call" | custom-call | tf_op jit(solution)/shard_map/pallas_call | solution.py:634
  91.1 1.9 %shard_map.106.heat = f32[8,128,128]{2,1,0:T(8,128)} custom-call(s32[8,128]{1,0:T(8,128)} %get-tuple-element.12.counts, s32[16,128]{1,0:T(8,128)} %get-tuple-element.13.lists, s32[680,128]{1,0:T(8,128)} %get-tuple-element.14.t, f32[680,128]{1,0:T(8,128)} %shard_map.105.f), custom_call_target="tpu_custom_call" | custom-call | tf_op jit(solution)/shard_map/pallas_call | solution.py:675
  93.0 2.6 %shard_map.107.state = f32[256,1024]{1,0:T(8,128)} custom-call(f32[8,128,128]{2,1,0:T(8,128)} %shard_map.106.heat, f32[256,1024]{1,0:T(8,128)} %get-tuple-element.18.t_fluid, f32[7,9,304,128]{3,2,1,0:T(8,128)} %get-tuple-element.19.ext), custom_call_target="tpu_custom_call" | custom-call | tf_op jit(solution)/shard_map/pallas_call | solution.py:808
  95.6 3.1 %shard_map.108 = (f32[680,128]{1,0:T(8,128)}, f32[256,1024]{1,0:T(8,128)}) custom-call(s32[8,128]{1,0:T(8,128)} %get-tuple-element.12.counts, s32[16,128]{1,0:T(8,128)} %get-tuple-element.13.lists, s32[680,128]{1,0:T(8,128)} %get-tuple-element.14.t, f32[256,1024]{1,0:T(8,128)} %shard_map.107.state), custom_call_target="tpu_custom_call" | custom-call | tf_op jit(solution)/shard_map/pallas_call | solution.py:716
  98.6 45.1 %shard_map.109 = f32[64,128]{1,0:T(8,128)} custom-call(f32[680,128]{1,0:T(8,128)} %get-tuple-element.21.values, s32[64,128]{1,0:T(8,128)} %get-tuple-element.16.pos1, s32[96,128]{1,0:T(8,128)} %get-tuple-element.17.pos2, f32[256,1024]{1,0:T(8,128)} %get-tuple-element.24.state, s32[64,128]{1,0:T(8,128)} %bitcast.8), custom_call_target="tpu_custom_call" | custom-call | tf_op jit(solution)/shard_map/pallas_call | solution.py:852
  143.7 1.4 copy.12

commit v6 on v5

--- a/solution.py
+++ b/solution.py
@@ -217,12 +217,17 @@
 
 
 def substeps(a, b, c, total, count):
+    def sweep(src, dst):
+        strips(lambda r: advance(src, dst, c, total, r), 2, 34, 17)
+
     def two(i, _):
-        strips(lambda r: advance(a, b, c, total, r), 1, 36, 12)
-        strips(lambda r: advance(b, a, c, total, r), 1, 36, 12)
+        sweep(a, b)
+        sweep(b, a)
         return 0
 
-    lax.fori_loop(0, count // 2, two, 0)
+    strips(lambda r: advance(a, b, c, total, r), 1, 36, 12)
+    sweep(b, a)
+    lax.fori_loop(1, count // 2, two, 0)
 
 
 def coefficients(e, c, low, high, r):
@@ -441,11 +446,11 @@
         strips(strip, 1, 36, 6)
 
     def maps(b, _):
-        s, k = lane_row(slot, b, 8), lane_row(coef, b, 8)
-        parts = split2(k) + split2(k * lane_row(prior, b, 8))
-        hit = iota((CY, 1024), 0) == (s >> 10)
+        s, k = lane_row(slot, b, 16), lane_row(coef, b, 16)
+        parts = split2(k) + split2(k * lane_row(prior, b, 16))
+        hit = iota((CY, 2048), 0) == (s >> 10)
         a = jnp.concatenate([jnp.where(hit, v, 0.0).astype(BF16) for v in parts], axis=0)
-        acc[...] += dot_nt(a, onehot(iota((CX, 1024), 0) == (s & 1023)))
+        acc[...] += dot_nt(a, onehot(iota((CX, 2048), 0) == (s & 1023)))
         return 0
 
     static, of_maps = halo_copies(0, 4, 0, pack, land), halo_copies(4, 2, 8, packm, landm)
@@ -481,11 +486,11 @@
     def _():
         pos1[...] = jnp.zeros_like(pos1)
 
-    lax.fori_loop(0, 4, maps, 0)
+    lax.fori_loop(0, 2, maps, 0)
 
     @pl.when(fluid)
     def _():
-        lax.fori_loop(4, 8, maps, 0)
+        lax.fori_loop(2, 4, maps, 0)
         place_maps()
 
     @pl.when(solid)
@@ -496,7 +501,7 @@
             compact(t, p2.at[i], t2.at[0, pl.ds(i * CROWS, CROWS)], o_ref, p_ref, t2_out)
             push(p2.at[i], p2_land, face_send.at[1], face_recv.at[1], (mine + i, blk))
         push(t2.at[0], t2.at[1], face_send.at[2], face_recv.at[2], (other, blk))
-        lax.fori_loop(4, 8, maps, 0)
+        lax.fori_loop(2, 4, maps, 0)
         place_maps()
 
     halo_start(of_maps, 4, 2, packm)
@@ -794,7 +799,7 @@
             warm(TILES - 1, last, jnp.where(iota((HALO, 128), 1) < 64, corner[0], corner[1]))
 
         for n in range(SOLID_STEPS - 1):
-            strips(lambda r: advance(e.at[n % 2], e.at[1 - n % 2], c, None, r), 1, 36, 12)
+            strips(lambda r: advance(e.at[n % 2], e.at[1 - n % 2], c, None, r), 2, 34, 17)
         done = [pltpu.make_async_copy(e.at[(SOLID_STEPS - 1) % 2, j, pl.ds(OY, CY)], t_out.at[:, pl.ds(128 * j, 128)], finish.at[j])
                 for j in range(TILES - 1)]
         for d in done:

time: 145 us -> 145 us (level)
  no operation moved by 1% of the time
where the time goes in v6:
time: 145 us
  Pallas kernels  143 us (99%)
    pallas_call x1, Pallas kernels, fluid(): pl.pallas_call(fluid_kernel, out_shape=[jax.ShapeDtypeStruct((CY, CX), F3...  61.1 us
    pallas_call x1, Pallas kernels, back(): pl.pallas_call(back_kernel, out_shape=jax.ShapeDtypeStruct((FROWS, 128),...  46 us
    pallas_call x1, Pallas kernels, face_flux(): pl.pallas_call(flux_kernel, out_shape=jax.ShapeDtypeStruct((2 * ALLP + 8,...  28.2 us
    pallas_call x1, Pallas kernels, wall_values(): pl.pallas_call(wall_kernel, in_specs=[sm, sm, vm, vm], out_specs=[vm, hbm...  3.06 us

profile of v6, /device:TPU:1, one launch (start us, length us, event | category | flops | bytes accessed | tf_op | source)
XLA Modules:
  0.0 145.1 jit_solution(7445480790888792366)
XLA Ops:
  0.6 61.1 %shard_map.104 = (f32[256,1024]{1,0:T(8,128)}, f32[8,256,128]{2,1,0:T(8,128)}, f32[7,9,304,128]{3,2,1,0:T(8,128)}, s32[64,128]{1,0:T(8,128)}, s32[96,128]{1,0:T(...) custom-call(f32[256,1024]{1,0:T(8,128)} %temp.1, f32[256,1024]{1,0:T(8,128)} %cond.1, ...), custom_call_target="tpu_custom_call" | custom-call | tf_op jit(solution)/shard_map/pallas_call | solution.py:560
  61.7 28.2 %shard_map.105.f = f32[680,128]{1,0:T(8,128)} custom-call(f32[8,256,128]{2,1,0:T(8,128)} %get-tuple-element.15.total, s32[64,128]{1,0:T(8,128)} %bitcast.7, f32[64,128]{1,0:T(8,128)} %bitcast.10, f32[64,128]{1,0:T(8,128)} %bitcast.12, s32[64,128]{1,0:T(8,128)} %get-tuple-element.16.pos1, s32[96,128]{1,0:T(8,128)} %get-tuple-element.17.pos2), custom_call_target="tpu_custom_call" | custom-call | tf_op jit(solution)/shard_map/pallas_call | solution.py:639
  89.9 2.2 %shard_map.106.heat = f32[8,128,128]{2,1,0:T(8,128)} custom-call(s32[8,128]{1,0:T(8,128)} %get-tuple-element.12.counts, s32[16,128]{1,0:T(8,128)} %get-tuple-element.13.lists, s32[680,128]{1,0:T(8,128)} %get-tuple-element.14.t, f32[680,128]{1,0:T(8,128)} %shard_map.105.f), custom_call_target="tpu_custom_call" | custom-call | tf_op jit(solution)/shard_map/pallas_call | solution.py:680
  92.1 2.6 %shard_map.107.state = f32[256,1024]{1,0:T(8,128)} custom-call(f32[8,128,128]{2,1,0:T(8,128)} %shard_map.106.heat, f32[256,1024]{1,0:T(8,128)} %get-tuple-element.18.t_fluid, f32[7,9,304,128]{3,2,1,0:T(8,128)} %get-tuple-element.19.ext), custom_call_target="tpu_custom_call" | custom-call | tf_op jit(solution)/shard_map/pallas_call | solution.py:813
  94.6 3.1 %shard_map.108 = (f32[680,128]{1,0:T(8,128)}, f32[256,1024]{1,0:T(8,128)}) custom-call(s32[8,128]{1,0:T(8,128)} %get-tuple-element.12.counts, s32[16,128]{1,0:T(8,128)} %get-tuple-element.13.lists, s32[680,128]{1,0:T(8,128)} %get-tuple-element.14.t, f32[256,1024]{1,0:T(8,128)} %shard_map.107.state), custom_call_target="tpu_custom_call" | custom-call | tf_op jit(solution)/shard_map/pallas_call | solution.py:721
  97.7 46.0 %shard_map.109 = f32[64,128]{1,0:T(8,128)} custom-call(f32[680,128]{1,0:T(8,128)} %get-tuple-element.21.values, s32[64,128]{1,0:T(8,128)} %get-tuple-element.16.pos1, s32[96,128]{1,0:T(8,128)} %get-tuple-element.17.pos2, f32[256,1024]{1,0:T(8,128)} %get-tuple-element.24.state, s32[64,128]{1,0:T(8,128)} %bitcast.8), custom_call_target="tpu_custom_call" | custom-call | tf_op jit(solution)/shard_map/pallas_call | solution.py:857
  143.7 1.4 copy.12
